TPU v7x, 512 devices: a whole 4x4x16 slice. The times are simulated.
512 devices in a mesh: width: 32 (over z, core), lat: 16 (over x, y).
Axes of the slice: x: 4, y: 4, z: 16, core: 2. Of those that a mesh axis runs over, the one named last changes fastest.
Arguments:
- residuals: bfloat16 [384, 16384], P(None, 'width'), may hold values from -6 to 6
- encoder: bfloat16 [16384, 16384], P('width', 'lat'), may hold values from -0.046875 to 0.046875
- enc_bias: float32 [16384], P('lat'), may hold values from -3 to 3
- decoder: bfloat16 [16384, 16384], P('lat', 'width'), may hold values from -0.046875 to 0.046875
- dec_bias: float32 [16384], P('width'), may hold values from -3 to 3
Outputs:
- enc_grad: bfloat16 [16384, 16384], P('width', 'lat')
- new_decoder: bfloat16 [16384, 16384], P('lat', 'width')
All inputs are finite; a program needn't handle non-finite values.
Results may differ from a plain program's by a relative error of at most 0.011.
Values may be sent and summed in bfloat16 or wider, within the bound.
No kernel may reach another device: no remote copies, remote signals or barrier semaphores. Data moves between devices by JAX's collectives and lax.ppermute only.
A program may use at most 64 MiB of HBM per device.

v0:
```python
import jax
import jax.numpy as jnp
from jax import lax
from jax.sharding import Mesh
from jax.sharding import PartitionSpec as P

WIDTH = ("width_0", "width_1")


EPS = 1e-06
STEP = 0.0003
PENALTY = 0.5


def split_up(shard, dim, count):
    dims = shard.shape
    tiles = shard.reshape(*dims[:dim], count, dims[dim] // count, *dims[dim + 1 :])
    return jnp.moveaxis(tiles, dim, 0)


def sum_at_owner(shard, axis, dim):
    tiles = split_up(shard, dim, lax.axis_size(axis))
    arrived = lax.all_to_all(tiles, axis, split_axis=0, concat_axis=0, tiled=True)
    return arrived.sum(axis=0)


def laid_out(tiles, dim):
    dims = list(tiles.shape[1:])
    dims[dim] *= tiles.shape[0]
    return jnp.moveaxis(tiles, 0, dim).reshape(dims)


def gather_in_order(shard, axes, order):
    tiles = shard
    for k in order:
        tiles = lax.all_gather(tiles, axes[k])
    done = order[::-1]
    back = [done.index(k) for k in range(len(axes))]
    tiles = tiles.transpose(*back, *range(len(axes), tiles.ndim))
    return tiles.reshape(-1, *shard.shape)


def whole_of(shard, axes, order, dim):
    return laid_out(gather_in_order(shard, axes, order), dim)


def sent_to_all(shard, axis):
    count = lax.axis_size(axis)
    return lax.all_to_all(
        jnp.broadcast_to(shard[None], (count, *shard.shape)), axis, 0, 0, tiled=True
    )


def gathered_copies(shard, axis, dim):
    return laid_out(sent_to_all(shard, axis), dim)


def over_copies(shard, axis):
    return sent_to_all(shard, axis).sum(axis=0)


def packed_total(arrays, axis):
    line, at, finished = (jnp.concatenate([a.reshape(-1) for a in arrays]), 0, [])
    running = over_copies(line, axis)
    for a in arrays:
        finished.append(running[at : at + a.size].reshape(a.shape))
        at += a.size
    return tuple(finished)


def per_device(residuals, encoder, enc_bias, decoder, dec_bias):
    tokens = residuals.shape[0]
    lat_count = lax.axis_size("lat")
    lat_rows = tokens // lat_count
    rows = residuals
    pre_rows = (
        sum_at_owner(jnp.dot(rows, encoder, preferred_element_type=jnp.float32), WIDTH, 0)
        + enc_bias
    )
    active_rows = pre_rows > 0.0
    act_rows = jnp.maximum(pre_rows, 0.0).astype(jnp.bfloat16)
    acts = whole_of(act_rows, WIDTH, (0, 1), 0)
    rows = acts
    recon_rows = sum_at_owner(jnp.dot(rows, decoder, preferred_element_type=jnp.float32), "lat", 0)
    first = lax.axis_index("lat") * lat_rows
    own_rows = lax.dynamic_slice_in_dim(residuals, first, lat_rows, 0)
    error_part = (recon_rows + dec_bias - own_rows.astype(jnp.float32)).astype(jnp.bfloat16)
    error = gathered_copies(error_part, "lat", 0)
    rows = error
    dacts_rows = (
        sum_at_owner(
            lax.dot_general(
                rows, decoder, (((1,), (1,)), ((), ())), preferred_element_type=jnp.float32
            ),
            WIDTH,
            0,
        )
        + PENALTY
    )
    dpre_part = jnp.where(active_rows, dacts_rows, 0.0).astype(jnp.bfloat16)
    dpre = whole_of(dpre_part, WIDTH, (0, 1), 0)
    enc_grad = lax.dot_general(
        residuals, dpre, (((0,), (0,)), ((), ())), preferred_element_type=jnp.float32
    ).astype(jnp.bfloat16)
    grad = lax.dot_general(
        acts, error, (((0,), (0,)), ((), ())), preferred_element_type=jnp.float32
    )
    weight = decoder.astype(jnp.float32)
    ww, gw, gg = packed_total(
        (
            jnp.sum(weight * weight, axis=1),
            jnp.sum(grad * weight, axis=1),
            jnp.sum(grad * grad, axis=1),
        ),
        WIDTH,
    )
    coef_row = gw / (ww + EPS)
    coef = coef_row[:, None]
    moved = weight - STEP * (grad - coef * weight)
    squared = (
        ww
        - 2.0 * STEP * (gw - coef_row * ww)
        + STEP * STEP * (gg - 2.0 * coef_row * gw + coef_row * coef_row * ww)
    )
    new_decoder = (moved / jnp.sqrt(squared + EPS)[:, None]).astype(jnp.bfloat16)
    return (enc_grad, new_decoder)


def solution(mesh):
    finer = Mesh(mesh.devices.reshape(16, 2, mesh.shape["lat"]), ("width_0", "width_1", "lat"))
    placed = (P(None, WIDTH), P(WIDTH, "lat"), P("lat"), P("lat", WIDTH), P(WIDTH))
    return jax.shard_map(
        per_device,
        mesh=finer,
        in_specs=placed,
        out_specs=(P(WIDTH, "lat"), P("lat", WIDTH)),
        check_vma=False,
    )
```

profile of v0, /device:TPU:1, one launch (start us, length us, event | category | flops | bytes accessed | tf_op | source)
XLA Modules:
  0.0 374.8 jit_solution(3232685895356255269)
XLA Ops:
  0.6 0.0 copy-start
  0.6 1.2 copy-done
  1.9 2.7 fusion.19
  4.6 1.4 reshape.103
  6.0 117.3 %all_to_all.26 = f32[32,12,1024]{2,1,0:T(8,128)} all-to-all(f32[32,12,1024]{2,1,0:T(8,128)S(1)} %reshape.103), channel_id=1, replica_groups=mesh['width_0'=16,'width_1'=2,'lat'=16] {'width_0','width_1'}, dimensions={0} | all-to-all | bytes 3145728 | tf_op jit(solution)/shard_map/all_to_all | solution.py:23
  123.4 0.0 copy-start.3
  123.4 1.7 reduce_sum.65
  125.1 0.0 copy-done.3
  125.1 0.0 copy-start.1
  125.1 22.3 %all_gather.20 = bf16[16,12,1024]{2,1,0:T(8,128)(2,1)S(1)} all-gather(bf16[1,12,1024]{2,1,0:T(8,128)(2,1)S(1)} %maximum_convert_fusion), channel_id=1, replica_groups=mesh['width_0'=16,'width_1'=2,'lat'=16] {'width_0'}, dimensions={0}, use_global_device_ids=true | all-gather | bytes 417792 | tf_op jit(solution)/shard_map/all_gather | solution.py:36
  147.5 0.2 copy.50
  147.7 9.4 %all-gather = bf16[32,12,1024]{2,0,1:T(8,128)(2,1)S(1)} all-gather(bf16[16,12,1024]{2,0,1:T(8,128)(2,1)S(1)} %copy.50), channel_id=2, replica_groups=mesh['width_0'=16,'width_1'=2,'lat'=16] {'width_1'}, dimensions={0}, use_global_device_ids=true | all-gather | bytes 1179648 | tf_op jit(solution)/shard_map/all_gather | solution.py:36
  157.1 0.1 copy.51
  157.2 0.0 copy-done.1
  157.2 0.0 copy-start.4
  157.2 1.6 fusion.9
  158.8 6.8 %all-to-all-start.1 = ((f32[16,24,512]{2,1,0:T(8,128)}), f32[16,24,512]{2,1,0:T(8,128)}, u32[]{:S(2)}, u32[]{:S(2)}) async-start(f32[16,24,512]{2,1,0:T(8,128)} %fusion.9), calls=%async_computation.1 | async-start | bytes 1572864 | tf_op jit(solution)/shard_map/all_to_all | solution.py:23
  165.6 12.8 %all-to-all-done.1 = f32[16,24,512]{2,1,0:T(8,128)} async-done(((f32[16,24,512]{2,1,0:T(8,128)}), f32[16,24,512]{2,1,0:T(8,128)}, u32[]{:S(2)}, u32[]{:S(2)}) %all-to-all-start.1) | async-done | bytes 786464 | tf_op jit(solution)/shard_map/all_to_all | solution.py:23
  178.4 1.2 reduce_sum.67
  179.6 0.0 copy-done.4
  179.6 0.8 subtract_convert_fusion
  180.4 0.8 broadcast_in_dim.5
  181.1 4.3 %all-to-all-start.2 = ((bf16[16,24,512]{2,1,0:T(8,128)(2,1)}), bf16[16,24,512]{2,1,0:T(8,128)(2,1)S(1)}, u32[]{:S(2)}, u32[]{:S(2)}) async-start(bf16[16,24,512]{2,1,0:T(8,128)(2,1)} %broadcast_in_dim.5), calls=%async_computation.2 | async-start | bytes 786432 | tf_op jit(solution)/shard_map/all_to_all | solution.py:49
  185.4 1.3 copy.57
  186.7 1.4 copy.58
  188.2 1.3 reshape_reshape.7
  189.5 3.9 %all-to-all-done.2 = bf16[16,24,512]{2,1,0:T(8,128)(2,1)S(1)} async-done(((bf16[16,24,512]{2,1,0:T(8,128)(2,1)}), bf16[16,24,512]{2,1,0:T(8,128)(2,1)S(1)}, u32[]{:S(2)}, u32[]{:S(2)}) %all-to-all-start.2) | async-done | bytes 393248 | tf_op jit(solution)/shard_map/all_to_all | solution.py:49
  193.4 3.4 fusion.1
  196.8 0.9 broadcast_in_dim.6
  197.8 8.3 %all-to-all-start.4 = ((f32[32,1,3072]{2,1,0:T(1,128)}), f32[32,1,3072]{2,1,0:T(1,128)}, u32[]{:S(2)}, u32[]{:S(2)}) async-start(f32[32,1,3072]{2,1,0:T(1,128)} %broadcast_in_dim.6), calls=%async_computation.4 | async-start | bytes 786432 | tf_op jit(solution)/shard_map/all_to_all | solution.py:49
  206.1 0.1 dot_general.22
  206.2 0.7 fusion.7
  206.9 2.2 copy.54
  209.1 25.0 %all-to-all-done.4 = f32[32,1,3072]{2,1,0:T(1,128)} async-done(((f32[32,1,3072]{2,1,0:T(1,128)}), f32[32,1,3072]{2,1,0:T(1,128)}, u32[]{:S(2)}, u32[]{:S(2)}) %all-to-all-start.4) | async-done | bytes 393248 | tf_op jit(solution)/shard_map/all_to_all | solution.py:49
  234.1 4.2 %all-to-all-start.3 = ((f32[32,12,1024]{2,1,0:T(8,128)}), f32[32,12,1024]{2,1,0:T(8,128)S(1)}, u32[]{:S(2)}, u32[]{:S(2)}) async-start(f32[32,12,1024]{2,1,0:T(8,128)} %copy.54), calls=%async_computation.3 | async-start | bytes 4194304 | tf_op jit(solution)/shard_map/all_to_all | solution.py:23
  238.3 1.2 reduce_sum.72
  239.5 3.3 fusion.5
  242.8 2.3 copy.61
  245.1 92.5 %all-to-all-done.3 = f32[32,12,1024]{2,1,0:T(8,128)S(1)} async-done(((f32[32,12,1024]{2,1,0:T(8,128)}), f32[32,12,1024]{2,1,0:T(8,128)S(1)}, u32[]{:S(2)}, u32[]{:S(2)}) %all-to-all-start.3) | async-done | bytes 1572896 | tf_op jit(solution)/shard_map/all_to_all | solution.py:23
  337.6 0.1 reduce_sum.68
  337.7 22.3 %all_gather.23 = bf16[16,12,1024]{2,1,0:T(8,128)(2,1)S(1)} all-gather(bf16[1,12,1024]{2,1,0:T(8,128)(2,1)S(1)} %fusion.13), channel_id=1, replica_groups=mesh['width_0'=16,'width_1'=2,'lat'=16] {'width_0'}, dimensions={0}, use_global_device_ids=true | all-gather | bytes 417792 | tf_op jit(solution)/shard_map/all_gather | solution.py:36
  360.1 0.2 copy.55
  360.3 11.4 %all-gather.1 = bf16[32,12,1024]{2,0,1:T(8,128)(2,1)S(1)} all-gather(bf16[16,12,1024]{2,0,1:T(8,128)(2,1)S(1)} %copy.55), channel_id=3, replica_groups=mesh['width_0'=16,'width_1'=2,'lat'=16] {'width_1'}, dimensions={0}, use_global_device_ids=true | all-gather | bytes 1179648 | tf_op jit(solution)/shard_map/all_gather | solution.py:36
  371.7 0.4 copy.71
  372.2 0.2 reshape_reshape.6
  372.3 0.4 copy-done.2
  372.7 0.7 fusion.6
  373.4 1.3 copy.60
  (5 shorter events, 0.0 us)
Async XLA Ops:
  0.6 1.2 copy-start
  123.4 1.7 copy-start.3
  125.1 32.1 %copy-start.1 = (bf16[1024,512]{1,0:T(8,128)(2,1)S(1)}, bf16[1024,512]{1,0:T(8,128)(2,1)}, u32[]{:S(2)}) copy-start(bf16[1024,512]{1,0:T(8,128)(2,1)} %param.8) | copy-start | bytes 3145732
  157.2 22.4 %copy-start.4 = (f32[512]{0:T(512)S(1)}, f32[512]{0:T(512)}, u32[]{:S(2)}) copy-start(f32[512]{0:T(512)} %param.9) | copy-start | bytes 6148
  158.8 19.6 %all-to-all-start.1 = ((f32[16,24,512]{2,1,0:T(8,128)}), f32[16,24,512]{2,1,0:T(8,128)}, u32[]{:S(2)}, u32[]{:S(2)}) async-start(f32[16,24,512]{2,1,0:T(8,128)} %fusion.9), calls=%async_computation.1 | async-start | bytes 1572864 | tf_op jit(solution)/shard_map/all_to_all | solution.py:23
  181.1 12.3 %all-to-all-start.2 = ((bf16[16,24,512]{2,1,0:T(8,128)(2,1)}), bf16[16,24,512]{2,1,0:T(8,128)(2,1)S(1)}, u32[]{:S(2)}, u32[]{:S(2)}) async-start(bf16[16,24,512]{2,1,0:T(8,128)(2,1)} %broadcast_in_dim.5), calls=%async_computation.2 | async-start | bytes 786432 | tf_op jit(solution)/shard_map/all_to_all | solution.py:49
  197.8 36.3 %all-to-all-start.4 = ((f32[32,1,3072]{2,1,0:T(1,128)}), f32[32,1,3072]{2,1,0:T(1,128)}, u32[]{:S(2)}, u32[]{:S(2)}) async-start(f32[32,1,3072]{2,1,0:T(1,128)} %broadcast_in_dim.6), calls=%async_computation.4 | async-start | bytes 786432 | tf_op jit(solution)/shard_map/all_to_all | solution.py:49
  234.1 103.5 %all-to-all-start.3 = ((f32[32,12,1024]{2,1,0:T(8,128)}), f32[32,12,1024]{2,1,0:T(8,128)S(1)}, u32[]{:S(2)}, u32[]{:S(2)}) async-start(f32[32,12,1024]{2,1,0:T(8,128)} %copy.54), calls=%async_computation.3 | async-start | bytes 4194304 | tf_op jit(solution)/shard_map/all_to_all | solution.py:23
  371.7 1.0 copy-start.2
where the time goes:
time: 376 us; the launch traced here: 375 us
  blocking collectives  183 us (49%)
  waiting for transfers between devices  134 us (36%)
  starting transfers between devices  23.5 us (6%)
  local copies, waits for them, and re-layouts  15.8 us (4%)
  matrix products  9.19 us (2%)
  other arithmetic  8.38 us (2%)
    all_to_all x1, blocking collectives, sum_at_owner(): lax.all_to_all(tiles, axis, split_axis=0, concat_axis=0, tiled=True)  117 us
    all_to_all x2, waiting for transfers between devices, sum_at_owner(): lax.all_to_all(tiles, axis, split_axis=0, concat_axis=0, tiled=True)  105 us
    all_gather x4, blocking collectives, gather_in_order(): tiles = lax.all_gather(tiles, axes[k])  65.5 us
    all_to_all x2, waiting for transfers between devices, sent_to_all(): lax.all_to_all(jnp.broadcast_to(shard[None], (count, *shard.shape)), axis...  29 us
    all_to_all x2, starting transfers between devices, sent_to_all(): lax.all_to_all(jnp.broadcast_to(shard[None], (count, *shard.shape)), axis...  12.6 us
    all_to_all x2, starting transfers between devices, sum_at_owner(): lax.all_to_all(tiles, axis, split_axis=0, concat_axis=0, tiled=True)  11 us
  transfers between devices with their start and end apart: 4, of which 4 were waited for; matrix products, arithmetic and copies ran while one was open for 4% of the time, Pallas kernels for 0%

commit v1 on v0

v1 whole, which is shorter than its diff:
```python
import jax
import jax.numpy as jnp
from jax import lax
from jax.sharding import Mesh
from jax.sharding import PartitionSpec as P

WIDTH = ("zhi", "zlo", "core")
STAGES = ("core", "zlo", "zhi")
F32, BF16 = jnp.float32, jnp.bfloat16

EPS = 1e-06
STEP = 0.0003
PENALTY = 0.5


def dot(a, b, contract):
    return lax.dot_general(a, b, (contract, ((), ())), preferred_element_type=F32)


def exchange(tiles, axis):
    return lax.all_to_all(tiles, axis, split_axis=0, concat_axis=0, tiled=True)


def sum_at_owner(shard, axis, sent):
    count = lax.axis_size(axis)
    tiles = shard.astype(sent).reshape(count, shard.shape[0] // count, *shard.shape[1:])
    return exchange(tiles, axis).astype(F32).sum(axis=0)


def staged_sum(shard, sent):
    for axis in STAGES:
        shard = sum_at_owner(shard, axis, sent)
    return shard


def sent_to_all(shard, axis):
    count = lax.axis_size(axis)
    tiles = exchange(jnp.broadcast_to(shard[None], (count, *shard.shape)), axis)
    return tiles.reshape(-1, *shard.shape[1:])


def per_device(residuals, encoder, enc_bias, decoder, dec_bias):
    tokens = residuals.shape[0]
    latents = encoder.shape[1]
    lat_rows = tokens // lax.axis_size("lat")
    pre = staged_sum(dot(encoder, residuals, ((0,), (1,))), F32)
    own = pre.shape[0]
    place = (lax.axis_index("core") * 4 + lax.axis_index("zlo")) * 4 + lax.axis_index("zhi")
    pre = pre + lax.dynamic_slice_in_dim(enc_bias, place * own, own)[:, None]
    active = pre > 0.0
    act = jnp.maximum(pre, 0.0).astype(BF16)
    acts = lax.all_gather(act, STAGES, tiled=True)
    recon = sum_at_owner(dot(acts, decoder, ((0,), (0,))), "lat", BF16)
    first = lax.axis_index("lat") * lat_rows
    own_rows = lax.dynamic_slice_in_dim(residuals, first, lat_rows, 0)
    error_part = (recon + dec_bias - own_rows.astype(F32)).astype(BF16)
    error = sent_to_all(error_part, "lat")
    dacts = staged_sum(dot(decoder, error, ((1,), (1,))), BF16) + PENALTY
    dpre_part = jnp.where(active, dacts, 0.0).astype(BF16)
    grad = dot(acts, error, ((1,), (0,)))
    weight = decoder.astype(F32)
    stats = jnp.stack(
        (
            jnp.sum(weight * weight, axis=1),
            jnp.sum(grad * weight, axis=1),
            jnp.sum(grad * grad, axis=1),
        )
    ).reshape(-1, tokens)
    carried = lax.all_gather(jnp.concatenate((dpre_part, stats.astype(BF16))), STAGES)
    dpre = carried[:, :own].reshape(latents, tokens)
    ww, gw, gg = carried[:, own:].astype(F32).sum(axis=0).reshape(3, latents)
    enc_grad = dot(residuals, dpre, ((0,), (1,))).astype(BF16)
    coef_row = gw / (ww + EPS)
    coef = coef_row[:, None]
    moved = weight - STEP * (grad - coef * weight)
    squared = (
        ww
        - 2.0 * STEP * (gw - coef_row * ww)
        + STEP * STEP * (gg - 2.0 * coef_row * gw + coef_row * coef_row * ww)
    )
    new_decoder = (moved / jnp.sqrt(squared + EPS)[:, None]).astype(BF16)
    return (enc_grad, new_decoder)


def solution(mesh):
    finer = Mesh(
        mesh.devices.reshape(4, 4, 2, mesh.shape["lat"]), ("zhi", "zlo", "core", "lat")
    )
    placed = (P(None, WIDTH), P(WIDTH, "lat"), P("lat"), P("lat", WIDTH), P(WIDTH))
    return jax.shard_map(
        per_device,
        mesh=finer,
        in_specs=placed,
        out_specs=(P(WIDTH, "lat"), P("lat", WIDTH)),
        check_vma=False,
    )
```

time: 376 us -> 338 us (0.90)
  waiting for transfers between devices: 134 us -> 38.4 us
  blocking collectives: 183 us -> 245 us
  local copies, waits for them, and re-layouts: 15.8 us -> 8.79 us
  starting transfers between devices: 23.5 us -> 30.5 us
  other arithmetic: 8.38 us -> 3.51 us
    all_gather x4 -> x2, blocking collectives: 65.5 us -> 192 us  [the longest x1 96.6 us: per_device(): lax.all_gather(jnp.concatenate((dpre_part, stats.astype(BF16))), STAGES)]
    all_to_all x4, waiting for transfers between devices: 134 us -> 38.4 us  [exchange(): return lax.all_to_all(tiles, axis, split_axis=0, concat_axis=0, tiled=True)]
    all_to_all x1 -> x4, blocking collectives: 117 us -> 52.9 us  [exchange(): return lax.all_to_all(tiles, axis, split_axis=0, concat_axis=0, tiled=True)]
    all_to_all x4, starting transfers between devices: 23.5 us -> 30.5 us  [exchange(): return lax.all_to_all(tiles, axis, split_axis=0, concat_axis=0, tiled=True)]
  transfers between devices with their start and end apart: 4 -> 4, of which waited for: 4 -> 4; matrix products, arithmetic and copies ran while one was open for 4% -> 2% of each run, Pallas kernels for 0% -> 0%
where the time goes in v1:
time: 338 us; the launch traced here: 337 us
  blocking collectives  245 us (72%)
  waiting for transfers between devices  38.4 us (11%)
  starting transfers between devices  30.5 us (9%)
  matrix products  10.4 us (3%)
  local copies, waits for them, and re-layouts  8.79 us (3%)
  other arithmetic  3.51 us (1%)
    all_gather x1, blocking collectives, per_device(): lax.all_gather(jnp.concatenate((dpre_part, stats.astype(BF16))), STAGES)  96.6 us
    all_gather x1, blocking collectives, per_device(): acts = lax.all_gather(act, STAGES, tiled=True)  95.1 us
    all_to_all x4, blocking collectives, exchange(): return lax.all_to_all(tiles, axis, split_axis=0, concat_axis=0, tiled=True)  52.9 us
    all_to_all x4, waiting for transfers between devices, exchange(): return lax.all_to_all(tiles, axis, split_axis=0, concat_axis=0, tiled=True)  38.4 us
    all_to_all x4, starting transfers between devices, exchange(): return lax.all_to_all(tiles, axis, split_axis=0, concat_axis=0, tiled=True)  30.5 us
    dot_general x5, matrix products, dot(): lax.dot_general(a, b, (contract, ((), ())), preferred_element_type=F32)  10.4 us
  transfers between devices with their start and end apart: 4, of which 4 were waited for; matrix products, arithmetic and copies ran while one was open for 2% of the time, Pallas kernels for 0%

profile of v1, /device:TPU:1, one launch (start us, length us, event | category | flops | bytes accessed | tf_op | source)
XLA Modules:
  0.0 336.9 jit_solution(12989903308994745471)
XLA Ops:
  0.6 0.0 copy-start
  0.6 1.2 copy-done
  1.9 1.7 fusion.8
  3.6 11.5 %all_to_all.40 = f32[2,512,384]{2,1,0:T(8,128)S(1)} all-to-all(f32[2,512,384]{2,1,0:T(8,128)S(1)} %bitcast.33), channel_id=1, replica_groups=mesh['zhi'=4,'zlo'=4,'core'=2,'lat'=16] {'core'}, dimensions={0} | all-to-all | bytes 3145728 | tf_op jit(solution)/shard_map/all_to_all | solution.py:21
  15.1 0.2 reduce_sum.105
  15.3 22.3 %all_to_all.41 = f32[4,128,384]{2,1,0:T(8,128)S(1)} all-to-all(f32[4,128,384]{2,1,0:T(8,128)S(1)} %bitcast.36), channel_id=1, replica_groups=mesh['zhi'=4,'zlo'=4,'core'=2,'lat'=16] {'zlo'}, dimensions={0} | all-to-all | bytes 1572864 | tf_op jit(solution)/shard_map/all_to_all | solution.py:21
  37.5 0.7 reduce_sum.106
  38.3 9.5 %all-to-all-start.2 = ((f32[4,32,384]{2,1,0:T(8,128)}), f32[4,32,384]{2,1,0:T(8,128)S(1)}, u32[]{:S(2)}, u32[]{:S(2)}) async-start(f32[4,32,384]{2,1,0:T(8,128)} %bitcast.2), calls=%async_computation.2 | async-start | bytes 393216 | tf_op jit(solution)/shard_map/all_to_all | solution.py:21
  47.8 0.8 dynamic_slice.6
  48.6 11.8 %all-to-all-done.2 = f32[4,32,384]{2,1,0:T(8,128)S(1)} async-done(((f32[4,32,384]{2,1,0:T(8,128)}), f32[4,32,384]{2,1,0:T(8,128)S(1)}, u32[]{:S(2)}, u32[]{:S(2)}) %all-to-all-start.2) | async-done | bytes 196640 | tf_op jit(solution)/shard_map/all_to_all | solution.py:21
  60.4 0.1 maximum_convert_fusion
  60.5 95.1 %all_gather.9 = bf16[1024,384]{1,0:T(8,128)(2,1)} all-gather(bf16[32,384]{1,0:T(8,128)(2,1)S(1)} %maximum_convert_fusion), channel_id=1, replica_groups=mesh['zhi'=4,'zlo'=4,'core'=2,'lat'=16] {'core','zlo','zhi'}, dimensions={0}, use_global_device_ids=true | all-gather | bytes 811008 | tf_op jit(solution)/shard_map/all_gather | solution.py:52
  155.5 0.0 copy-start.1
  155.5 0.0 copy-start.3
  155.5 0.0 copy-start.2
  155.5 2.9 convolution_convert_fusion.2
  158.4 6.7 %all-to-all-start.3 = ((bf16[16,24,512]{2,1,0:T(8,128)(2,1)}), bf16[16,24,512]{2,1,0:T(8,128)(2,1)S(1)}, u32[]{:S(2)}, u32[]{:S(2)}) async-start(bf16[16,24,512]{2,1,0:T(8,128)(2,1)} %bitcast.3), calls=%async_computation.3 | async-start | bytes 786432 | tf_op jit(solution)/shard_map/all_to_all | solution.py:21
  165.2 8.2 %all-to-all-done.3 = bf16[16,24,512]{2,1,0:T(8,128)(2,1)S(1)} async-done(((bf16[16,24,512]{2,1,0:T(8,128)(2,1)}), bf16[16,24,512]{2,1,0:T(8,128)(2,1)S(1)}, u32[]{:S(2)}, u32[]{:S(2)}) %all-to-all-start.3) | async-done | bytes 393248 | tf_op jit(solution)/shard_map/all_to_all | solution.py:21
  173.4 0.1 convert_reduce_fusion
  173.5 0.0 copy-done.1
  173.5 0.0 copy-done.3
  173.6 11.9 %all_to_all.42 = bf16[16,24,512]{2,1,0:T(8,128)(2,1)S(1)} all-to-all(bf16[16,24,512]{2,1,0:T(8,128)(2,1)S(1)} %broadcast_in_dim.3), channel_id=1, replica_groups=mesh['zhi'=4,'zlo'=4,'core'=2,'lat'=16] {'lat'}, dimensions={0} | all-to-all | bytes 786432 | tf_op jit(solution)/shard_map/all_to_all | solution.py:21
  185.4 0.0 copy-done.2
  185.5 0.6 convolution_convert_fusion.1
  186.1 0.1 copy.44
  186.1 7.3 %all_to_all.43 = bf16[2,512,384]{1,2,0:T(8,128)(2,1)S(1)} all-to-all(bf16[2,512,384]{1,2,0:T(8,128)(2,1)S(1)} %bitcast.38), channel_id=1, replica_groups=mesh['zhi'=4,'zlo'=4,'core'=2,'lat'=16] {'core'}, dimensions={0} | all-to-all | bytes 1572864 | tf_op jit(solution)/shard_map/all_to_all | solution.py:21
  193.4 0.2 reduce_sum.109
  193.6 0.8 copy_bitcast_fusion.1
  194.4 6.8 %all-to-all-start.6 = ((bf16[4,128,384]{1,2,0:T(8,128)(2,1)}), bf16[4,128,384]{1,2,0:T(8,128)(2,1)S(1)}, u32[]{:S(2)}, u32[]{:S(2)}) async-start(bf16[4,128,384]{1,2,0:T(8,128)(2,1)} %copy_bitcast_fusion.1), calls=%async_computation.6 | async-start | bytes 786432 | tf_op jit(solution)/shard_map/all_to_all | solution.py:21
  201.2 1.5 copy.35
  202.7 9.7 %all-to-all-done.6 = bf16[4,128,384]{1,2,0:T(8,128)(2,1)S(1)} async-done(((bf16[4,128,384]{1,2,0:T(8,128)(2,1)}), bf16[4,128,384]{1,2,0:T(8,128)(2,1)S(1)}, u32[]{:S(2)}, u32[]{:S(2)}) %all-to-all-start.6) | async-done | bytes 393248 | tf_op jit(solution)/shard_map/all_to_all | solution.py:21
  212.4 0.1 reduce_sum.110
  212.5 0.8 copy.34
  213.3 7.4 %all-to-all-start.7 = ((bf16[4,32,384]{2,1,0:T(8,128)(2,1)}), bf16[4,32,384]{2,1,0:T(8,128)(2,1)S(1)}, u32[]{:S(2)}, u32[]{:S(2)}) async-start(bf16[4,32,384]{2,1,0:T(8,128)(2,1)} %bitcast.6), calls=%async_computation.7 | async-start | bytes 196608 | tf_op jit(solution)/shard_map/all_to_all | solution.py:21
  220.6 3.3 fusion.1
  224.0 8.6 %all-to-all-done.7 = bf16[4,32,384]{2,1,0:T(8,128)(2,1)S(1)} async-done(((bf16[4,32,384]{2,1,0:T(8,128)(2,1)}), bf16[4,32,384]{2,1,0:T(8,128)(2,1)S(1)}, u32[]{:S(2)}, u32[]{:S(2)}) %all-to-all-start.7) | async-done | bytes 98336 | tf_op jit(solution)/shard_map/all_to_all | solution.py:21
  232.6 0.1 select_convert_fusion
  232.7 96.6 %all-gather = bf16[1280,384]{1,0:T(8,128)(2,1)S(1)} all-gather(bf16[40,384]{1,0:T(8,128)(2,1)S(1)} %pad_maximum_fusion), channel_id=2, replica_groups=mesh['zhi'=4,'zlo'=4,'core'=2,'lat'=16] {'core','zlo','zhi'}, dimensions={0}, use_global_device_ids=true | all-gather | bytes 1013760 | tf_op jit(solution)/shard_map/all_gather | solution.py:69
  329.3 1.0 slice.8
  330.3 2.1 fusion.5
  332.4 1.3 copy.37
  333.7 1.8 fusion.6
  335.6 1.3 copy.36
  (14 shorter events, 0.2 us)
Async XLA Ops:
  0.6 1.2 copy-start
  38.3 22.1 %all-to-all-start.2 = ((f32[4,32,384]{2,1,0:T(8,128)}), f32[4,32,384]{2,1,0:T(8,128)S(1)}, u32[]{:S(2)}, u32[]{:S(2)}) async-start(f32[4,32,384]{2,1,0:T(8,128)} %bitcast.2), calls=%async_computation.2 | async-start | bytes 393216 | tf_op jit(solution)/shard_map/all_to_all | solution.py:21
  155.5 18.0 %copy-start.1 = (bf16[384,512]{1,0:T(8,128)(2,1)S(1)}, bf16[384,512]{1,0:T(8,128)(2,1)}, u32[]{:S(2)}) copy-start(bf16[384,512]{1,0:T(8,128)(2,1)} %param.5) | copy-start | bytes 1179652
  155.5 18.0 %copy-start.3 = (f32[512]{0:T(512)S(1)}, f32[512]{0:T(512)}, u32[]{:S(2)}) copy-start(f32[512]{0:T(512)} %param.9) | copy-start | bytes 6148
  155.5 29.9 %copy-start.2 = (bf16[1024,512]{1,0:T(8,128)(2,1)S(1)}, bf16[1024,512]{1,0:T(8,128)(2,1)}, u32[]{:S(2)}) copy-start(bf16[1024,512]{1,0:T(8,128)(2,1)} %param.8) | copy-start | bytes 3145732
  158.4 15.0 %all-to-all-start.3 = ((bf16[16,24,512]{2,1,0:T(8,128)(2,1)}), bf16[16,24,512]{2,1,0:T(8,128)(2,1)S(1)}, u32[]{:S(2)}, u32[]{:S(2)}) async-start(bf16[16,24,512]{2,1,0:T(8,128)(2,1)} %bitcast.3), calls=%async_computation.3 | async-start | bytes 786432 | tf_op jit(solution)/shard_map/all_to_all | solution.py:21
  194.4 18.0 %all-to-all-start.6 = ((bf16[4,128,384]{1,2,0:T(8,128)(2,1)}), bf16[4,128,384]{1,2,0:T(8,128)(2,1)S(1)}, u32[]{:S(2)}, u32[]{:S(2)}) async-start(bf16[4,128,384]{1,2,0:T(8,128)(2,1)} %copy_bitcast_fusion.1), calls=%async_computation.6 | async-start | bytes 786432 | tf_op jit(solution)/shard_map/all_to_all | solution.py:21
  213.3 19.4 %all-to-all-start.7 = ((bf16[4,32,384]{2,1,0:T(8,128)(2,1)}), bf16[4,32,384]{2,1,0:T(8,128)(2,1)S(1)}, u32[]{:S(2)}, u32[]{:S(2)}) async-start(bf16[4,32,384]{2,1,0:T(8,128)(2,1)} %bitcast.6), calls=%async_computation.7 | async-start | bytes 196608 | tf_op jit(solution)/shard_map/all_to_all | solution.py:21

commit v2 on v1

--- a/solution.py
+++ b/solution.py
@@ -28,6 +28,9 @@
 
 
 def staged_sum(shard, sent):
+    sizes = [lax.axis_size(axis) for axis in WIDTH]
+    tiles = shard.astype(sent).reshape(*sizes, -1, shard.shape[1])
+    shard = tiles.transpose(2, 1, 0, 3, 4).reshape(shard.shape)
     for axis in STAGES:
         shard = sum_at_owner(shard, axis, sent)
     return shard
@@ -45,11 +48,11 @@
     lat_rows = tokens // lax.axis_size("lat")
     pre = staged_sum(dot(encoder, residuals, ((0,), (1,))), F32)
     own = pre.shape[0]
-    place = (lax.axis_index("core") * 4 + lax.axis_index("zlo")) * 4 + lax.axis_index("zhi")
+    place = lax.axis_index(WIDTH)
     pre = pre + lax.dynamic_slice_in_dim(enc_bias, place * own, own)[:, None]
     active = pre > 0.0
     act = jnp.maximum(pre, 0.0).astype(BF16)
-    acts = lax.all_gather(act, STAGES, tiled=True)
+    acts = lax.all_gather(act, WIDTH, tiled=True)
     recon = sum_at_owner(dot(acts, decoder, ((0,), (0,))), "lat", BF16)
     first = lax.axis_index("lat") * lat_rows
     own_rows = lax.dynamic_slice_in_dim(residuals, first, lat_rows, 0)
@@ -66,7 +69,7 @@
             jnp.sum(grad * grad, axis=1),
         )
     ).reshape(-1, tokens)
-    carried = lax.all_gather(jnp.concatenate((dpre_part, stats.astype(BF16))), STAGES)
+    carried = lax.all_gather(jnp.concatenate((dpre_part, stats.astype(BF16))), WIDTH)
     dpre = carried[:, :own].reshape(latents, tokens)
     ww, gw, gg = carried[:, own:].astype(F32).sum(axis=0).reshape(3, latents)
     enc_grad = dot(residuals, dpre, ((0,), (1,))).astype(BF16)

time: 338 us -> 213 us (0.63)
  blocking collectives: 245 us -> 122 us
  starting transfers between devices: 30.5 us -> 24.9 us
    all_gather x2, blocking collectives: 192 us -> 69.7 us  [the longest x1 37.3 us: per_device(): acts = lax.all_gather(act, WIDTH, tiled=True)]
    all_to_all x4, starting transfers between devices: 30.5 us -> 24.9 us  [exchange(): return lax.all_to_all(tiles, axis, split_axis=0, concat_axis=0, tiled=True)]
  transfers between devices with their start and end apart: 4 -> 4, of which waited for: 4 -> 4; matrix products, arithmetic and copies ran while one was open for 2% -> 3% of each run, Pallas kernels for 0% -> 0%
where the time goes in v2:
time: 213 us; the launch traced here: 212 us
  blocking collectives  122 us (57%)
  waiting for transfers between devices  39.8 us (19%)
  starting transfers between devices  24.9 us (12%)
  matrix products  11.3 us (5%)
  local copies, waits for them, and re-layouts  8.89 us (4%)
  other arithmetic  4.97 us (2%)
    all_to_all x4, blocking collectives, exchange(): return lax.all_to_all(tiles, axis, split_axis=0, concat_axis=0, tiled=True)  51.9 us
    all_to_all x4, waiting for transfers between devices, exchange(): return lax.all_to_all(tiles, axis, split_axis=0, concat_axis=0, tiled=True)  39.8 us
    all_gather x1, blocking collectives, per_device(): acts = lax.all_gather(act, WIDTH, tiled=True)  37.3 us
    all_gather x1, blocking collectives, per_device(): lax.all_gather(jnp.concatenate((dpre_part, stats.astype(BF16))), WIDTH)  32.4 us
    all_to_all x4, starting transfers between devices, exchange(): return lax.all_to_all(tiles, axis, split_axis=0, concat_axis=0, tiled=True)  24.9 us
    dot_general x5, matrix products, dot(): lax.dot_general(a, b, (contract, ((), ())), preferred_element_type=F32)  11.3 us
    unnamed x11, local copies, waits for them, and re-layouts  5.36 us
  transfers between devices with their start and end apart: 4, of which 4 were waited for; matrix products, arithmetic and copies ran while one was open for 3% of the time, Pallas kernels for 0%

profile of v2, /device:TPU:1, one launch (start us, length us, event | category | flops | bytes accessed | tf_op | source)
XLA Modules:
  0.0 212.3 jit_solution(1244220649667766184)
XLA Ops:
  0.6 0.0 copy-start
  0.6 1.2 copy-done
  1.9 1.7 fusion.9
  3.6 0.1 copy.16
  3.7 11.5 %all_to_all.40 = f32[2,512,384]{2,1,0:T(8,128)S(1)} all-to-all(f32[2,512,384]{2,1,0:T(8,128)S(1)} %bitcast.33), channel_id=1, replica_groups=mesh['zhi'=4,'zlo'=4,'core'=2,'lat'=16] {'core'}, dimensions={0} | all-to-all | bytes 3145728 | tf_op jit(solution)/shard_map/all_to_all | solution.py:21
  15.2 0.2 reduce_sum.105
  15.4 22.3 %all_to_all.41 = f32[4,128,384]{2,1,0:T(8,128)S(1)} all-to-all(f32[4,128,384]{2,1,0:T(8,128)S(1)} %bitcast.37), channel_id=1, replica_groups=mesh['zhi'=4,'zlo'=4,'core'=2,'lat'=16] {'zlo'}, dimensions={0} | all-to-all | bytes 1572864 | tf_op jit(solution)/shard_map/all_to_all | solution.py:21
  37.7 0.7 reduce_sum.106
  38.4 9.5 %all-to-all-start.2 = ((f32[4,32,384]{2,1,0:T(8,128)}), f32[4,32,384]{2,1,0:T(8,128)S(1)}, u32[]{:S(2)}, u32[]{:S(2)}) async-start(f32[4,32,384]{2,1,0:T(8,128)} %bitcast.4), calls=%async_computation.2 | async-start | bytes 393216 | tf_op jit(solution)/shard_map/all_to_all | solution.py:21
  47.9 0.8 dynamic_slice.6
  48.7 11.8 %all-to-all-done.2 = f32[4,32,384]{2,1,0:T(8,128)S(1)} async-done(((f32[4,32,384]{2,1,0:T(8,128)}), f32[4,32,384]{2,1,0:T(8,128)S(1)}, u32[]{:S(2)}, u32[]{:S(2)}) %all-to-all-start.2) | async-done | bytes 196640 | tf_op jit(solution)/shard_map/all_to_all | solution.py:21
  60.5 0.1 maximum_convert_fusion
  60.6 37.3 %all_gather.9 = bf16[1024,384]{1,0:T(8,128)(2,1)} all-gather(bf16[32,384]{1,0:T(8,128)(2,1)S(1)} %maximum_convert_fusion), channel_id=1, replica_groups=mesh['zhi'=4,'zlo'=4,'core'=2,'lat'=16] {'zhi','zlo','core'}, dimensions={0}, use_global_device_ids=true | all-gather | bytes 811008 | tf_op jit(solution)/shard_map/all_gather | solution.py:55
  97.9 0.0 copy-start.1
  97.9 0.0 copy-start.3
  97.9 0.0 copy-start.2
  97.9 2.9 %convolution_convert_fusion.2 = bf16[384,512]{1,0:T(8,128)(2,1)} fusion(bf16[1024,384]{1,0:T(8,128)(2,1)} %all_gather.9, bf16[1024,512]{1,0:T(8,128)(2,1)} %param.8), kind=kOutput, calls=%fused_computation.15 | convolution fusion | flops 402849792 | bytes 2228224 | tf_op jit(solution)/shard_map/dot_general | solution.py:17
  100.8 6.7 %all-to-all-start.3 = ((bf16[16,24,512]{2,1,0:T(8,128)(2,1)}), bf16[16,24,512]{2,1,0:T(8,128)(2,1)S(1)}, u32[]{:S(2)}, u32[]{:S(2)}) async-start(bf16[16,24,512]{2,1,0:T(8,128)(2,1)} %bitcast.5), calls=%async_computation.3 | async-start | bytes 786432 | tf_op jit(solution)/shard_map/all_to_all | solution.py:21
  107.6 9.3 %all-to-all-done.3 = bf16[16,24,512]{2,1,0:T(8,128)(2,1)S(1)} async-done(((bf16[16,24,512]{2,1,0:T(8,128)(2,1)}), bf16[16,24,512]{2,1,0:T(8,128)(2,1)S(1)}, u32[]{:S(2)}, u32[]{:S(2)}) %all-to-all-start.3) | async-done | bytes 393248 | tf_op jit(solution)/shard_map/all_to_all | solution.py:21
  116.9 0.1 convert_reduce_fusion
  116.9 0.0 copy-done.1
  116.9 0.0 copy-done.3
  117.0 11.5 %all_to_all.42 = bf16[16,24,512]{2,1,0:T(8,128)(2,1)S(1)} all-to-all(bf16[16,24,512]{2,1,0:T(8,128)(2,1)S(1)} %broadcast_in_dim.3), channel_id=1, replica_groups=mesh['zhi'=4,'zlo'=4,'core'=2,'lat'=16] {'lat'}, dimensions={0} | all-to-all | bytes 786432 | tf_op jit(solution)/shard_map/all_to_all | solution.py:21
  128.5 0.0 copy-done.2
  128.5 1.5 fusion.7
  130.0 1.5 copy.17
  131.5 0.1 copy.18
  131.6 6.6 %all_to_all.43 = bf16[2,512,384]{2,1,0:T(8,128)(2,1)S(1)} all-to-all(bf16[2,512,384]{2,1,0:T(8,128)(2,1)S(1)} %bitcast.40), channel_id=1, replica_groups=mesh['zhi'=4,'zlo'=4,'core'=2,'lat'=16] {'core'}, dimensions={0} | all-to-all | bytes 1572864 | tf_op jit(solution)/shard_map/all_to_all | solution.py:21
  138.3 1.0 reduce_sum.109
  139.2 3.5 %all-to-all-start.6 = ((bf16[4,128,384]{2,1,0:T(8,128)(2,1)}), bf16[4,128,384]{2,1,0:T(8,128)(2,1)S(1)}, u32[]{:S(2)}, u32[]{:S(2)}) async-start(bf16[4,128,384]{2,1,0:T(8,128)(2,1)} %bitcast.11), calls=%async_computation.6 | async-start | bytes 786432 | tf_op jit(solution)/shard_map/all_to_all | solution.py:21
  142.7 1.5 copy.19
  144.2 9.9 %all-to-all-done.6 = bf16[4,128,384]{2,1,0:T(8,128)(2,1)S(1)} async-done(((bf16[4,128,384]{2,1,0:T(8,128)(2,1)}), bf16[4,128,384]{2,1,0:T(8,128)(2,1)S(1)}, u32[]{:S(2)}, u32[]{:S(2)}) %all-to-all-start.6) | async-done | bytes 393248 | tf_op jit(solution)/shard_map/all_to_all | solution.py:21
  154.1 0.7 reduce_sum.110
  154.8 5.2 %all-to-all-start.7 = ((bf16[4,32,384]{2,1,0:T(8,128)(2,1)}), bf16[4,32,384]{2,1,0:T(8,128)(2,1)S(1)}, u32[]{:S(2)}, u32[]{:S(2)}) async-start(bf16[4,32,384]{2,1,0:T(8,128)(2,1)} %bitcast.12), calls=%async_computation.7 | async-start | bytes 196608 | tf_op jit(solution)/shard_map/all_to_all | solution.py:21
  160.0 3.3 %fusion.1 = (bf16[1024]{0:T(1024)(128)(2,1)S(1)}, bf16[1024]{0:T(1024)(128)(2,1)S(1)}, bf16[1024]{0:T(1024)(128)(2,1)S(1)}, f32[1024,512]{0,1:T(8,128)}) fusion(bf16[1024,512]{0,1:T(8,128)(2,1)S(1)} %copy.19, bf16[1024,384]{1,0:T(8,128)(2,1)} %all_gather.9, bf16[384,512]{1,0:T(8,128)(2,1)S(1)} %bitcast.42), kind=kOutput, calls=%fused_computation.5 | convolution fusion | flops 406320128 | bytes 4331520 | tf_op jit(solution)/shard_map/dot_general | solution.py:17
  163.4 8.7 %all-to-all-done.7 = bf16[4,32,384]{2,1,0:T(8,128)(2,1)S(1)} async-done(((bf16[4,32,384]{2,1,0:T(8,128)(2,1)}), bf16[4,32,384]{2,1,0:T(8,128)(2,1)S(1)}, u32[]{:S(2)}, u32[]{:S(2)}) %all-to-all-start.7) | async-done | bytes 98336 | tf_op jit(solution)/shard_map/all_to_all | solution.py:21
  172.2 0.1 select_convert_fusion
  172.3 32.4 %all-gather = bf16[1280,384]{1,0:T(8,128)(2,1)S(1)} all-gather(bf16[40,384]{1,0:T(8,128)(2,1)S(1)} %pad_maximum_fusion), channel_id=2, replica_groups=mesh['zhi'=4,'zlo'=4,'core'=2,'lat'=16] {'zhi','zlo','core'}, dimensions={0}, use_global_device_ids=true | all-gather | bytes 1013760 | tf_op jit(solution)/shard_map/all_gather | solution.py:72
  204.7 1.0 slice.8
  205.7 2.1 fusion.5
  207.8 1.3 copy.21
  209.1 1.8 fusion.6
  211.0 1.3 copy.20
  (14 shorter events, 0.2 us)
Async XLA Ops:
  0.6 1.2 copy-start
  38.4 22.1 %all-to-all-start.2 = ((f32[4,32,384]{2,1,0:T(8,128)}), f32[4,32,384]{2,1,0:T(8,128)S(1)}, u32[]{:S(2)}, u32[]{:S(2)}) async-start(f32[4,32,384]{2,1,0:T(8,128)} %bitcast.4), calls=%async_computation.2 | async-start | bytes 393216 | tf_op jit(solution)/shard_map/all_to_all | solution.py:21
  97.9 19.1 %copy-start.1 = (bf16[384,512]{1,0:T(8,128)(2,1)S(1)}, bf16[384,512]{1,0:T(8,128)(2,1)}, u32[]{:S(2)}) copy-start(bf16[384,512]{1,0:T(8,128)(2,1)} %param.5) | copy-start | bytes 1179652
  97.9 19.1 %copy-start.3 = (f32[512]{0:T(512)S(1)}, f32[512]{0:T(512)}, u32[]{:S(2)}) copy-start(f32[512]{0:T(512)} %param.9) | copy-start | bytes 6148
  97.9 30.7 %copy-start.2 = (bf16[1024,512]{1,0:T(8,128)(2,1)S(1)}, bf16[1024,512]{1,0:T(8,128)(2,1)}, u32[]{:S(2)}) copy-start(bf16[1024,512]{1,0:T(8,128)(2,1)} %param.8) | copy-start | bytes 3145732
  100.8 16.1 %all-to-all-start.3 = ((bf16[16,24,512]{2,1,0:T(8,128)(2,1)}), bf16[16,24,512]{2,1,0:T(8,128)(2,1)S(1)}, u32[]{:S(2)}, u32[]{:S(2)}) async-start(bf16[16,24,512]{2,1,0:T(8,128)(2,1)} %bitcast.5), calls=%async_computation.3 | async-start | bytes 786432 | tf_op jit(solution)/shard_map/all_to_all | solution.py:21
  139.2 14.9 %all-to-all-start.6 = ((bf16[4,128,384]{2,1,0:T(8,128)(2,1)}), bf16[4,128,384]{2,1,0:T(8,128)(2,1)S(1)}, u32[]{:S(2)}, u32[]{:S(2)}) async-start(bf16[4,128,384]{2,1,0:T(8,128)(2,1)} %bitcast.11), calls=%async_computation.6 | async-start | bytes 786432 | tf_op jit(solution)/shard_map/all_to_all | solution.py:21
  154.8 17.4 %all-to-all-start.7 = ((bf16[4,32,384]{2,1,0:T(8,128)(2,1)}), bf16[4,32,384]{2,1,0:T(8,128)(2,1)S(1)}, u32[]{:S(2)}, u32[]{:S(2)}) async-start(bf16[4,32,384]{2,1,0:T(8,128)(2,1)} %bitcast.12), calls=%async_computation.7 | async-start | bytes 196608 | tf_op jit(solution)/shard_map/all_to_all | solution.py:21

commit v3 on v2

v3 whole, which is shorter than its diff:
```python
import functools

import jax
import jax.numpy as jnp
from jax import lax
from jax.experimental import pallas as pl
from jax.experimental.pallas import tpu as pltpu
from jax.sharding import Mesh
from jax.sharding import PartitionSpec as P

WIDTH = ("zhi", "zlo", "core")
F32, BF16 = jnp.float32, jnp.bfloat16
LANES = 128

EPS = 1e-06
STEP = 0.0003
PENALTY = 0.5


def dot(a, b, contract):
    return lax.dot_general(a, b, (contract, ((), ())), preferred_element_type=F32)


def exchange(tiles, axis):
    return lax.all_to_all(tiles, axis, split_axis=0, concat_axis=0, tiled=True)


def sum_at_owner(shard, axis):
    count = lax.axis_size(axis)
    tiles = shard.reshape(count, shard.shape[0] // count, *shard.shape[1:])
    return exchange(tiles, axis).astype(F32).sum(axis=0)


def staged_sum(shard, stages, sent):
    for stage in stages:
        shard = sum_at_owner(shard.astype(sent), stage)
    return shard


def sent_to_all(shard, axis):
    count = lax.axis_size(axis)
    tiles = exchange(jnp.broadcast_to(shard[None], (count, *shard.shape)), axis)
    return tiles.reshape(-1, *shard.shape[1:])


def own_block(array, axis):
    rows = array.shape[0] // lax.axis_size(axis)
    return lax.dynamic_slice_in_dim(array, lax.axis_index(axis) * rows, rows, 0)


def whole_in_vmem(body, outs, operands, flops):
    size = sum(a.size * a.dtype.itemsize for a in (*operands, *outs))
    spec = pl.BlockSpec(memory_space=pltpu.VMEM)
    return pl.pallas_call(
        body,
        out_shape=outs,
        in_specs=[spec] * len(operands),
        out_specs=[spec] * len(outs),
        compiler_params=pltpu.CompilerParams(vmem_limit_bytes=16 * 2**20),
        cost_estimate=pl.CostEstimate(flops=flops, bytes_accessed=size, transcendentals=0),
    )(*operands)


def product_body(left, right, out):
    out[...] = dot(left[...], right[...], ((1,), (0,))).astype(out.dtype)


def dacts_body(decoder, error, out):
    cores, zs, own = out.shape[:3]
    step = 4
    for first in range(0, zs, step):
        rows = decoder[first * cores * own : (first + step) * cores * own, :]
        part = dot(rows, error[...], ((1,), (0,))).astype(BF16)
        for z in range(step):
            for core in range(cores):
                at = (z * cores + core) * own
                out[core, first + z] = part[at : at + own, :]


def grad_body(acts, error, decoder, grad, stats):
    for r in range(acts.shape[0] // LANES):
        rows = slice(r * LANES, (r + 1) * LANES)
        part = dot(acts[rows, :], error[...], ((1,), (1,)))
        grad[rows, :] = part
        weight = decoder[rows, :].astype(F32)
        for k, product in enumerate((weight * weight, part * weight, part * part)):
            folded = product[:, :LANES]
            for c in range(LANES, product.shape[1], LANES):
                folded = folded + product[:, c : c + LANES]
            line = jnp.sum(folded.T, axis=0, keepdims=True)
            stats[r : r + 1, k * LANES : (k + 1) * LANES] = line


def final_body(own, inputs, carried, stats, grad, decoder, enc_grad, new_decoder):
    count = carried.shape[0]
    step = 8
    for first in range(0, count, step):
        rows = carried[first : first + step, :own, :].reshape(step * own, carried.shape[2])
        columns = slice(first * own, (first + step) * own)
        enc_grad[:, columns] = dot(inputs[...], rows, ((1,), (1,))).astype(BF16)
    ww, gw, gg = (stats[:, k * LANES : (k + 1) * LANES] for k in range(3))
    coef = gw / (ww + EPS)
    squared = (
        ww
        - 2.0 * STEP * (gw - coef * ww)
        + STEP * STEP * (gg - 2.0 * coef * gw + coef * coef * ww)
    )
    scale = lax.rsqrt(squared + EPS)
    of_weight = scale * (1.0 + STEP * coef)
    of_grad = scale * STEP
    for r in range(stats.shape[0]):
        rows = slice(r * LANES, (r + 1) * LANES)
        a, b = (
            jnp.broadcast_to(t[r : r + 1, :], (LANES, LANES)).T for t in (of_weight, of_grad)
        )
        for c in range(0, grad.shape[1], LANES):
            at = (rows, slice(c, c + LANES))
            new_decoder[at] = (a * decoder[at].astype(F32) - b * grad[at]).astype(BF16)


def per_device(residuals, encoder, enc_bias, decoder, dec_bias):
    tokens, depth = residuals.shape
    latents = encoder.shape[1]
    sizes = [lax.axis_size(axis) for axis in WIDTH]
    own = latents // lax.axis_size(WIDTH)
    flops = 2 * tokens * depth * latents
    inputs, turned = lax.optimization_barrier((residuals.T, decoder.T))
    partial = dot(encoder, residuals, ((0,), (1,))).reshape(*sizes, own, tokens)
    partial = partial.transpose(2, 1, 0, 3, 4).reshape(latents, tokens)
    pre = staged_sum(partial, ("core", "zlo", "zhi"), F32)
    pre = pre + own_block(enc_bias, WIDTH)[:, None]
    active = pre > 0.0
    act = jnp.maximum(pre, 0.0).astype(BF16)
    acts = lax.all_gather(act, WIDTH, tiled=True)
    (recon,) = whole_in_vmem(
        product_body, [jax.ShapeDtypeStruct((depth, tokens), BF16)], (turned, acts), flops
    )
    recon = sum_at_owner(recon, "lat")
    target = own_block(inputs, "lat").astype(F32)
    error_part = (recon + own_block(dec_bias, "lat")[:, None] - target).astype(BF16)
    error = sent_to_all(error_part, "lat")
    zs = sizes[0] * sizes[1]
    (partial,) = whole_in_vmem(
        dacts_body,
        [jax.ShapeDtypeStruct((sizes[2], zs, own, tokens), BF16)],
        (decoder, error),
        flops,
    )
    dacts = staged_sum(partial.reshape(latents, tokens), ("core", ("zhi", "zlo")), BF16) + PENALTY
    dpre_part = jnp.where(active, dacts, 0.0).astype(BF16)
    groups = latents // LANES
    grad, stats = whole_in_vmem(
        grad_body,
        [
            jax.ShapeDtypeStruct((latents, depth), F32),
            jax.ShapeDtypeStruct((groups, 3 * LANES), F32),
        ],
        (acts, error, decoder),
        flops,
    )
    carried = lax.all_gather(jnp.concatenate((dpre_part, stats.astype(BF16))), WIDTH)
    stats = carried[:, own:].astype(F32).sum(axis=0)
    enc_grad, new_decoder = whole_in_vmem(
        functools.partial(final_body, own),
        [
            jax.ShapeDtypeStruct((depth, latents), BF16),
            jax.ShapeDtypeStruct((latents, depth), BF16),
        ],
        (inputs, carried, stats, grad, decoder),
        flops,
    )
    return (enc_grad, new_decoder)


def solution(mesh):
    finer = Mesh(
        mesh.devices.reshape(4, 4, 2, mesh.shape["lat"]), ("zhi", "zlo", "core", "lat")
    )
    placed = (P(None, WIDTH), P(WIDTH, "lat"), P("lat"), P("lat", WIDTH), P(WIDTH))
    return jax.shard_map(
        per_device,
        mesh=finer,
        in_specs=placed,
        out_specs=(P(WIDTH, "lat"), P("lat", WIDTH)),
        check_vma=False,
    )
```

time: 213 us -> 210 us (0.986)
  matrix products: 11.3 us -> 1.75 us
  blocking collectives: 122 us -> 130 us
  waiting for transfers between devices: 39.8 us -> 33.7 us
  Pallas kernels: 0 us -> 4.78 us
  starting transfers between devices: 24.9 us -> 21.6 us
  other arithmetic: 4.97 us -> 7.98 us
    dot_general x5 -> x1, matrix products: 11.3 us -> 1.75 us  [dot(): lax.dot_general(a, b, (contract, ((), ())), preferred_element_type=F32)]
    all_gather x1, blocking collectives: 32.4 us -> 40.8 us  [per_device(): lax.all_gather(jnp.concatenate((dpre_part, stats.astype(BF16))), WIDTH)]
    all_to_all x4 -> x3, waiting for transfers between devices: 39.8 us -> 33.7 us  [exchange(): return lax.all_to_all(tiles, axis, split_axis=0, concat_axis=0, tiled=True)]
    reduce_sum x7 -> x6, other arithmetic: 2.64 us -> 7.7 us  [sum_at_owner(): return exchange(tiles, axis).astype(F32).sum(axis=0)]
    pallas_call x0 -> x4, Pallas kernels: none -> 4.78 us  [whole_in_vmem(): pl.pallas_call(body, out_shape=outs, in_specs=[spec] * len(operands), out...]
    all_to_all x4 -> x3, starting transfers between devices: 24.9 us -> 21.6 us  [exchange(): return lax.all_to_all(tiles, axis, split_axis=0, concat_axis=0, tiled=True)]
    all_gather x1, blocking collectives: 37.3 us -> 34.4 us  [per_device(): acts = lax.all_gather(act, WIDTH, tiled=True)]
    all_to_all x4, blocking collectives: 51.9 us -> 54.4 us  [exchange(): return lax.all_to_all(tiles, axis, split_axis=0, concat_axis=0, tiled=True)]
  transfers between devices with their start and end apart: 4 -> 3, of which waited for: 4 -> 3; matrix products, arithmetic and copies ran while one was open for 3% -> 1% of each run, Pallas kernels for 0% -> 1%
where the time goes in v3:
time: 210 us; the launch traced here: 209 us
  blocking collectives  130 us (62%)
  waiting for transfers between devices  33.7 us (16%)
  starting transfers between devices  21.6 us (10%)
  local copies, waits for them, and re-layouts  9.34 us (4%)
  other arithmetic  7.98 us (4%)
  Pallas kernels  4.78 us (2%)
    all_to_all x4, blocking collectives, exchange(): return lax.all_to_all(tiles, axis, split_axis=0, concat_axis=0, tiled=True)  54.4 us
    all_gather x1, blocking collectives, per_device(): lax.all_gather(jnp.concatenate((dpre_part, stats.astype(BF16))), WIDTH)  40.8 us
    all_gather x1, blocking collectives, per_device(): acts = lax.all_gather(act, WIDTH, tiled=True)  34.4 us
    all_to_all x3, waiting for transfers between devices, exchange(): return lax.all_to_all(tiles, axis, split_axis=0, concat_axis=0, tiled=True)  33.7 us
    all_to_all x3, starting transfers between devices, exchange(): return lax.all_to_all(tiles, axis, split_axis=0, concat_axis=0, tiled=True)  21.6 us
    reduce_sum x6, other arithmetic, sum_at_owner(): return exchange(tiles, axis).astype(F32).sum(axis=0)  7.7 us
    unnamed x20, local copies, waits for them, and re-layouts  7.66 us
    pallas_call x4, Pallas kernels, whole_in_vmem(): pl.pallas_call(body, out_shape=outs, in_specs=[spec] * len(operands), out...  4.78 us
  transfers between devices with their start and end apart: 3, of which 3 were waited for; matrix products, arithmetic and copies ran while one was open for 1% of the time, Pallas kernels for 1%

profile of v3, /device:TPU:1, one launch (start us, length us, event | category | flops | bytes accessed | tf_op | source)
XLA Modules:
  0.0 209.5 jit_solution(8621739212389940606)
XLA Ops:
  0.6 0.0 copy-start
  0.6 1.2 copy-done
  1.9 1.7 fusion
  3.6 0.1 copy.14
  3.7 12.3 %all_to_all.35 = f32[2,512,384]{2,1,0:T(8,128)} all-to-all(f32[2,512,384]{2,1,0:T(8,128)S(1)} %bitcast.24), channel_id=1, replica_groups=mesh['zhi'=4,'zlo'=4,'core'=2,'lat'=16] {'core'}, dimensions={0} | all-to-all | bytes 3145728 | tf_op jit(solution)/shard_map/all_to_all | solution.py:25
  16.1 1.6 reduce_sum.66
  17.7 0.0 copy-start.8
  17.7 0.0 copy-start.1
  17.7 23.1 %all_to_all.36 = f32[4,128,384]{2,1,0:T(8,128)} all-to-all(f32[4,128,384]{2,1,0:T(8,128)S(1)} %bitcast.26), channel_id=1, replica_groups=mesh['zhi'=4,'zlo'=4,'core'=2,'lat'=16] {'zlo'}, dimensions={0} | all-to-all | bytes 1572864 | tf_op jit(solution)/shard_map/all_to_all | solution.py:25
  40.8 1.9 reduce_sum.67
  42.7 9.4 %all-to-all-start.2 = ((f32[4,32,384]{2,1,0:T(8,128)}), f32[4,32,384]{2,1,0:T(8,128)S(1)}, u32[]{:S(2)}, u32[]{:S(2)}) async-start(f32[4,32,384]{2,1,0:T(8,128)} %bitcast.6), calls=%async_computation.2 | async-start | bytes 393216 | tf_op jit(solution)/shard_map/all_to_all | solution.py:25
  52.1 0.0 copy-done.8
  52.1 0.2 copy.12
  52.3 0.0 copy-start.5
  52.3 0.0 copy-done.1
  52.3 1.3 copy.13
  53.7 0.8 dynamic_slice.9
  54.4 10.5 %all-to-all-done.2 = f32[4,32,384]{2,1,0:T(8,128)S(1)} async-done(((f32[4,32,384]{2,1,0:T(8,128)}), f32[4,32,384]{2,1,0:T(8,128)S(1)}, u32[]{:S(2)}, u32[]{:S(2)}) %all-to-all-start.2) | async-done | bytes 196640 | tf_op jit(solution)/shard_map/all_to_all | solution.py:25
  64.9 0.1 maximum_convert_fusion
  65.0 34.4 %all_gather.9.right.acts = bf16[1024,384]{1,0:T(8,128)(2,1)S(1)} all-gather(bf16[32,384]{1,0:T(8,128)(2,1)S(1)} %maximum_convert_fusion), channel_id=1, replica_groups=mesh['zhi'=4,'zlo'=4,'core'=2,'lat'=16] {'zhi','zlo','core'}, dimensions={0}, use_global_device_ids=true | all-gather | bytes 811008 | tf_op jit(solution)/shard_map/all_gather | solution.py:134
  99.4 0.0 copy-start.2
  99.4 1.2 copy-done.2
  100.6 0.7 shard_map.68
  101.3 0.0 copy-start.7
  101.3 0.7 copy-done.7
  102.0 6.8 %all-to-all-start.3 = ((bf16[16,32,384]{2,1,0:T(8,128)(2,1)}), bf16[16,32,384]{2,1,0:T(8,128)(2,1)}, u32[]{:S(2)}, u32[]{:S(2)}) async-start(bf16[16,32,384]{2,1,0:T(8,128)(2,1)} %bitcast.23), calls=%async_computation.3 | async-start | bytes 786432 | tf_op jit(solution)/shard_map/all_to_all | solution.py:25
  108.9 0.8 dynamic_slice.10
  109.6 8.6 %all-to-all-done.3 = bf16[16,32,384]{2,1,0:T(8,128)(2,1)} async-done(((bf16[16,32,384]{2,1,0:T(8,128)(2,1)}), bf16[16,32,384]{2,1,0:T(8,128)(2,1)}, u32[]{:S(2)}, u32[]{:S(2)}) %all-to-all-start.3) | async-done | bytes 393248 | tf_op jit(solution)/shard_map/all_to_all | solution.py:25
  118.2 1.1 convert_reduce_fusion.1
  119.3 0.0 copy-done.5
  119.3 0.1 subtract_convert_fusion
  119.4 11.6 %all_to_all.37 = bf16[16,32,384]{2,1,0:T(8,128)(2,1)S(1)} all-to-all(bf16[16,32,384]{2,1,0:T(8,128)(2,1)S(1)} %broadcast_in_dim.3), channel_id=1, replica_groups=mesh['zhi'=4,'zlo'=4,'core'=2,'lat'=16] {'lat'}, dimensions={0} | all-to-all | bytes 786432 | tf_op jit(solution)/shard_map/all_to_all | solution.py:25
  131.0 0.7 shard_map.69
  131.7 7.4 %all_to_all.38 = bf16[2,512,384]{2,1,0:T(8,128)(2,1)} all-to-all(bf16[2,512,384]{2,1,0:T(8,128)(2,1)S(1)} %bitcast.20), channel_id=1, replica_groups=mesh['zhi'=4,'zlo'=4,'core'=2,'lat'=16] {'core'}, dimensions={0} | all-to-all | bytes 1572864 | tf_op jit(solution)/shard_map/all_to_all | solution.py:25
  139.1 2.1 %reduce_sum.70 = bf16[512,384]{1,0:T(8,128)(2,1)} reduce(bf16[2,512,384]{2,1,0:T(8,128)(2,1)} %all_to_all.38, bf16[]{:T(256)} %constant.36.clone.1), dimensions={0}, to_apply=%region_4.0 | reduce | flops 196608 | bytes 1179650 | tf_op jit(solution)/shard_map/reduce_sum | solution.py:31
  141.2 5.3 %all-to-all-start.6 = ((bf16[16,32,384]{2,1,0:T(8,128)(2,1)}), bf16[16,32,384]{2,1,0:T(8,128)(2,1)}, u32[]{:S(2)}, u32[]{:S(2)}) async-start(bf16[16,32,384]{2,1,0:T(8,128)(2,1)} %bitcast.27), calls=%async_computation.6 | async-start | bytes 786432 | tf_op jit(solution)/shard_map/all_to_all | solution.py:25
  146.5 1.2 shard_map.70
  147.8 0.0 copy-start.3
  147.8 1.3 copy-done.3
  149.1 0.0 copy-start.6
  149.1 14.6 %all-to-all-done.6 = bf16[16,32,384]{2,1,0:T(8,128)(2,1)} async-done(((bf16[16,32,384]{2,1,0:T(8,128)(2,1)}), bf16[16,32,384]{2,1,0:T(8,128)(2,1)}, u32[]{:S(2)}, u32[]{:S(2)}) %all-to-all-start.6) | async-done | bytes 393248 | tf_op jit(solution)/shard_map/all_to_all | solution.py:25
  163.8 1.1 convert_reduce_fusion
  164.8 0.1 select_convert_fusion
  164.9 40.8 %all-gather = bf16[1280,384]{1,0:T(8,128)(2,1)S(1)} all-gather(bf16[40,384]{1,0:T(8,128)(2,1)S(1)} %pad_maximum_fusion), channel_id=2, replica_groups=mesh['zhi'=4,'zlo'=4,'core'=2,'lat'=16] {'zhi','zlo','core'}, dimensions={0}, use_global_device_ids=true | all-gather | bytes 1013760 | tf_op jit(solution)/shard_map/all_gather | solution.py:161
  205.7 0.0 copy-done.6
  205.7 0.0 copy-start.4
  205.7 1.6 copy-done.4
  207.3 2.1 %shard_map.71 = (bf16[512,1024]{1,0:T(8,128)(2,1)}, bf16[1024,512]{1,0:T(8,128)(2,1)}) custom-call(bf16[512,384]{1,0:T(8,128)(2,1)S(1)} %bitcast.22, bf16[32,40,384]{2,1,0:T(8,128)(2,1)S(1)} %bitcast.16, f32[8,384]{1,0:T(8,128)S(1)} %convert_reduce_fusion.2.stats, f32[1024,512]{1,0:T(8,128)S(1)} %copy-done.4, bf16[1024,512]{1,0:T(8,128)(2,1)S(1)} %copy-done.1), custom_call_target="tpu_custom_call" | custom-call | flops 402653184 | bytes 6631424 | tf_op jit(solution)/shard_map/pallas_call | solution.py:54
  (5 shorter events, 0.1 us)
Async XLA Ops:
  0.6 1.2 copy-start
  17.7 34.4 %copy-start.8 = (bf16[384,512]{1,0:T(8,128)(2,1)S(1)}, bf16[384,512]{1,0:T(8,128)(2,1)}, u32[]{:S(2)}) copy-start(bf16[384,512]{1,0:T(8,128)(2,1)} %param.5) | copy-start | bytes 1179652
  17.7 34.7 %copy-start.1 = (bf16[1024,512]{1,0:T(8,128)(2,1)S(1)}, bf16[1024,512]{1,0:T(8,128)(2,1)}, u32[]{:S(2)}) copy-start(bf16[1024,512]{1,0:T(8,128)(2,1)} %decoder.5) | copy-start | bytes 3145732
  42.7 22.2 %all-to-all-start.2 = ((f32[4,32,384]{2,1,0:T(8,128)}), f32[4,32,384]{2,1,0:T(8,128)S(1)}, u32[]{:S(2)}, u32[]{:S(2)}) async-start(f32[4,32,384]{2,1,0:T(8,128)} %bitcast.6), calls=%async_computation.2 | async-start | bytes 393216 | tf_op jit(solution)/shard_map/all_to_all | solution.py:25
  52.3 67.0 %copy-start.5 = (bf16[384,512]{0,1:T(8,128)(2,1)}, bf16[384,512]{0,1:T(8,128)(2,1)S(1)}, u32[]{:S(2)}) copy-start(bf16[384,512]{0,1:T(8,128)(2,1)S(1)} %copy.12) | copy-start | bytes 1179652
  99.4 1.2 copy-start.2
  101.3 0.7 copy-start.7
  102.0 16.2 %all-to-all-start.3 = ((bf16[16,32,384]{2,1,0:T(8,128)(2,1)}), bf16[16,32,384]{2,1,0:T(8,128)(2,1)}, u32[]{:S(2)}, u32[]{:S(2)}) async-start(bf16[16,32,384]{2,1,0:T(8,128)(2,1)} %bitcast.23), calls=%async_computation.3 | async-start | bytes 786432 | tf_op jit(solution)/shard_map/all_to_all | solution.py:25
  141.2 22.6 %all-to-all-start.6 = ((bf16[16,32,384]{2,1,0:T(8,128)(2,1)}), bf16[16,32,384]{2,1,0:T(8,128)(2,1)}, u32[]{:S(2)}, u32[]{:S(2)}) async-start(bf16[16,32,384]{2,1,0:T(8,128)(2,1)} %bitcast.27), calls=%async_computation.6 | async-start | bytes 786432 | tf_op jit(solution)/shard_map/all_to_all | solution.py:25
  147.8 1.4 copy-start.3
  149.1 56.6 %copy-start.6 = (bf16[384,512]{0,1:T(8,128)(2,1)S(1)}, bf16[384,512]{0,1:T(8,128)(2,1)}, u32[]{:S(2)}) copy-start(bf16[384,512]{0,1:T(8,128)(2,1)} %copy-done.5) | copy-start | bytes 1179652
  205.7 1.6 copy-start.4

commit v4 on v3

v4 whole, which is shorter than its diff:
```python
import functools

import jax
import jax.numpy as jnp
from jax import lax
from jax.experimental import pallas as pl
from jax.experimental.pallas import tpu as pltpu
from jax.sharding import Mesh
from jax.sharding import PartitionSpec as P

WIDTH = ("zhi", "zlo", "core")
NEAR = ("zlo", "core")
F32, BF16 = jnp.float32, jnp.bfloat16
LANES = 128

EPS = 1e-06
STEP = 0.0003
PENALTY = 0.5


def dot(a, b, contract):
    return lax.dot_general(a, b, (contract, ((), ())), preferred_element_type=F32)


def exchange(tiles, axis):
    return lax.all_to_all(tiles, axis, split_axis=0, concat_axis=0, tiled=True)


def total(tiles):
    result = tiles[0].astype(F32)
    for k in range(1, tiles.shape[0]):
        result = result + tiles[k].astype(F32)
    return result


def total_body(tiles, out):
    out[...] = total(tiles).astype(out.dtype)


def sum_of(tiles):
    out = jax.ShapeDtypeStruct(tiles.shape[1:], tiles.dtype)
    return whole_in_vmem(total_body, [out], [tiles], tiles.size)[0]


def split_exchange(shard, axis):
    count = lax.axis_size(axis)
    tiles = shard.reshape(count, shard.shape[0] // count, *shard.shape[1:])
    return exchange(tiles, axis)


def own_block(array, axis):
    rows = array.shape[0] // lax.axis_size(axis)
    return lax.dynamic_slice_in_dim(array, lax.axis_index(axis) * rows, rows, 0)


def whole_in_vmem(body, outs, operands, flops, scratch=()):
    size = sum(a.size * a.dtype.itemsize for a in (*operands, *outs))
    spec = pl.BlockSpec(memory_space=pltpu.VMEM)
    return pl.pallas_call(
        body,
        out_shape=outs,
        in_specs=[spec] * len(operands),
        out_specs=[spec] * len(outs),
        scratch_shapes=scratch,
        compiler_params=pltpu.CompilerParams(vmem_limit_bytes=16 * 2**20),
        cost_estimate=pl.CostEstimate(flops=flops, bytes_accessed=size, transcendentals=0),
    )(*operands)


def product_body(left, right, out):
    out[...] = dot(left[...], right[...], ((1,), (0,))).astype(out.dtype)


def act_body(tiles, bias, act, active):
    pre = total(tiles) + bias[...]
    act[...] = jnp.maximum(pre, 0.0).astype(BF16)
    active[...] = jnp.where(pre > 0.0, 1.0, 0.0)


def error_body(tiles, offset, out):
    error = (total(tiles) + offset[...]).astype(BF16)
    for k in range(out.shape[0]):
        out[k] = error


def dacts_body(decoder, error, out):
    cores, zs, own = out.shape[:3]
    for z in range(zs):
        rows = decoder[z * cores * own : (z + 1) * cores * own, :]
        part = dot(rows, error[...], ((1,), (0,))).astype(BF16)
        for core in range(cores):
            out[core, z] = part[core * own : (core + 1) * own, :]


def in_two(sums):
    high = sums.astype(BF16).astype(F32)
    return jnp.concatenate((high, sums - high)).astype(BF16)


def from_two(rows):
    half = rows.shape[0] // 2
    return rows[:half] + rows[half:]


def grad_body(acts, error, decoder, grad, stats, sums):
    for r in range(acts.shape[0] // LANES):
        rows = slice(r * LANES, (r + 1) * LANES)
        part = dot(acts[rows, :], error[...], ((1,), (1,)))
        grad[rows, :] = part
        weight = decoder[rows, :].astype(F32)
        for k, product in enumerate((weight * weight, part * weight, part * part)):
            folded = product[:, :LANES]
            for c in range(LANES, product.shape[1], LANES):
                folded = folded + product[:, c : c + LANES]
            line = jnp.sum(folded.T, axis=0, keepdims=True)
            sums[r : r + 1, k * LANES : (k + 1) * LANES] = line
    stats[...] = in_two(sums[...])


def joined_body(tiles, stats, out):
    own = tiles.shape[1]
    out[:own, :] = total(tiles).astype(BF16)
    out[own:, :] = stats[...]


def dpre_body(tiles, active, out):
    own = active.shape[0]
    sums = total(tiles)
    dacts = sums[:own] + PENALTY
    out[:own, :] = jnp.where(active[...] > 0.0, dacts, 0.0).astype(BF16)
    out[own:, :] = in_two(from_two(sums[own:]))


def final_body(own, inputs, carried, grad, decoder, enc_grad, new_decoder):
    count, _, tokens = carried.shape
    step = 2
    for first in range(0, count, step):
        rows = carried[first : first + step, :own, :].reshape(step * own, tokens)
        columns = slice(first * own, (first + step) * own)
        enc_grad[:, columns] = dot(inputs[...], rows, ((1,), (1,))).astype(BF16)
    stats = carried[0, own:, :].astype(F32)
    for k in range(1, count):
        stats = stats + carried[k, own:, :].astype(F32)
    stats = from_two(stats)
    ww, gw, gg = (stats[:, k * LANES : (k + 1) * LANES] for k in range(3))
    coef = gw / (ww + EPS)
    squared = (
        ww
        - 2.0 * STEP * (gw - coef * ww)
        + STEP * STEP * (gg - 2.0 * coef * gw + coef * coef * ww)
    )
    scale = lax.rsqrt(squared + EPS)
    of_weight = scale * (1.0 + STEP * coef)
    of_grad = scale * STEP
    for r in range(stats.shape[0]):
        rows = slice(r * LANES, (r + 1) * LANES)
        a, b = (
            jnp.broadcast_to(t[r : r + 1, :], (LANES, LANES)).T for t in (of_weight, of_grad)
        )
        for c in range(0, grad.shape[1], LANES):
            at = (rows, slice(c, c + LANES))
            new_decoder[at] = (a * decoder[at].astype(F32) - b * grad[at]).astype(BF16)


def per_device(residuals, encoder, enc_bias, decoder, dec_bias):
    tokens, depth = residuals.shape
    latents = encoder.shape[1]
    zs, cores = lax.axis_size("zlo"), lax.axis_size("core")
    own = latents // (zs * cores)
    flops = 2 * tokens * depth * latents
    shape = jax.ShapeDtypeStruct
    inputs, turned = lax.optimization_barrier((residuals.T, decoder.T))

    partial = dot(encoder, residuals, ((0,), (1,))).reshape(zs, cores, own, tokens)
    partial = partial.transpose(1, 0, 2, 3).reshape(latents, tokens)
    pre = sum_of(split_exchange(partial, "core"))
    pre = sum_of(split_exchange(pre, "zlo"))
    act, active = whole_in_vmem(
        act_body,
        [shape(pre.shape, BF16), shape(pre.shape, F32)],
        (lax.all_gather(pre, "zhi"), own_block(enc_bias, NEAR)[:, None]),
        pre.size,
    )
    acts = lax.all_gather(act, NEAR, tiled=True)

    (recon,) = whole_in_vmem(product_body, [shape((depth, tokens), BF16)], (turned, acts), flops)
    tiles = split_exchange(recon, "lat")
    offset = own_block(dec_bias, "lat")[:, None] - own_block(inputs, "lat").astype(F32)
    (copies,) = whole_in_vmem(
        error_body, [shape(tiles.shape, BF16)], (tiles, offset), tiles.size
    )
    error = exchange(copies, "lat").reshape(depth, tokens)

    (partial,) = whole_in_vmem(
        dacts_body, [shape((cores, zs, own, tokens), BF16)], (decoder, error), flops
    )
    grad, stats = whole_in_vmem(
        grad_body,
        [shape((latents, depth), F32), shape((2 * latents // LANES, 3 * LANES), BF16)],
        (acts, error, decoder),
        flops,
        [pltpu.VMEM((latents // LANES, 3 * LANES), F32)],
    )
    half = sum_of(exchange(partial.reshape(cores, zs * own, tokens), "core"))
    tiles = split_exchange(half, "zlo")
    both = shape((own + stats.shape[0], tokens), BF16)
    (joined,) = whole_in_vmem(joined_body, [both], (tiles, stats), tiles.size)
    (dpre,) = whole_in_vmem(
        dpre_body, [both], (lax.all_gather(joined, "zhi"), active), 4 * joined.size
    )
    carried = lax.all_gather(dpre, NEAR)
    enc_grad, new_decoder = whole_in_vmem(
        functools.partial(final_body, own),
        [shape((depth, latents), BF16), shape((latents, depth), BF16)],
        (inputs, carried, grad, decoder),
        flops,
    )
    return (enc_grad, new_decoder)


def solution(mesh):
    finer = Mesh(
        mesh.devices.reshape(4, 4, 2, mesh.shape["lat"]), ("zhi", "zlo", "core", "lat")
    )
    placed = (P(None, WIDTH), P(WIDTH, "lat"), P("lat"), P("lat", WIDTH), P(WIDTH))
    return jax.shard_map(
        per_device,
        mesh=finer,
        in_specs=placed,
        out_specs=(P(WIDTH, "lat"), P("lat", WIDTH)),
        check_vma=False,
    )
```

time: 210 us -> 191 us (0.910)
  other arithmetic: 7.98 us -> 0.07 us
  starting transfers between devices: 21.6 us -> 14.1 us
  blocking collectives: 130 us -> 124 us
  Pallas kernels: 4.78 us -> 7.44 us
    all_to_all x4 -> x3, blocking collectives: 54.4 us -> 29.7 us  [exchange(): return lax.all_to_all(tiles, axis, split_axis=0, concat_axis=0, tiled=True)]
    all_gather x2 -> x4, blocking collectives: 75.2 us -> 93.8 us  [the longest x1 34.5 us: per_device(): lax.all_gather(pre, 'zhi')]
    reduce_sum x7 -> x0, other arithmetic: 7.74 us -> none  [the longest x6 7.7 us: sum_at_owner(): return exchange(tiles, axis).astype(F32).sum(axis=0)]
    all_to_all x3, starting transfers between devices: 21.6 us -> 14.1 us  [exchange(): return lax.all_to_all(tiles, axis, split_axis=0, concat_axis=0, tiled=True)]
    pallas_call x4 -> x11, Pallas kernels: 4.78 us -> 7.44 us  [whole_in_vmem(): pl.pallas_call(body, out_shape=outs, in_specs=[spec] * len(operands), out...]
    unnamed x20 -> x22, local copies, waits for them, and re-layouts: 7.66 us -> 7.46 us
  transfers between devices with their start and end apart: 3 -> 3, of which waited for: 3 -> 3; matrix products, arithmetic and copies ran while one was open for 1% -> 2% of each run, Pallas kernels for 1% -> 1%
where the time goes in v4:
time: 191 us
  blocking collectives  124 us (65%)
  waiting for transfers between devices  33.8 us (18%)
  starting transfers between devices  14.1 us (7%)
  local copies, waits for them, and re-layouts  9.26 us (5%)
  Pallas kernels  7.44 us (4%)
    all_gather x1, blocking collectives, per_device(): lax.all_gather(pre, 'zhi')  34.5 us
    all_to_all x3, waiting for transfers between devices, exchange(): return lax.all_to_all(tiles, axis, split_axis=0, concat_axis=0, tiled=True)  33.8 us
    all_to_all x3, blocking collectives, exchange(): return lax.all_to_all(tiles, axis, split_axis=0, concat_axis=0, tiled=True)  29.7 us
    all_gather x1, blocking collectives, per_device(): lax.all_gather(joined, 'zhi')  21.3 us
    all_gather x1, blocking collectives, per_device(): carried = lax.all_gather(dpre, NEAR)  20.3 us
    all_gather x1, blocking collectives, per_device(): acts = lax.all_gather(act, NEAR, tiled=True)  17.7 us
    all_to_all x3, starting transfers between devices, exchange(): return lax.all_to_all(tiles, axis, split_axis=0, concat_axis=0, tiled=True)  14.1 us
    unnamed x22, local copies, waits for them, and re-layouts  7.46 us
  transfers between devices with their start and end apart: 3, of which 3 were waited for; matrix products, arithmetic and copies ran while one was open for 2% of the time, Pallas kernels for 1%

profile of v4, /device:TPU:1, one launch (start us, length us, event | category | flops | bytes accessed | tf_op | source)
XLA Modules:
  0.0 190.7 jit_solution(10322013485019444891)
XLA Ops:
  0.6 0.0 copy-start
  0.6 1.2 copy-done
  1.9 1.7 fusion
  3.6 0.1 copy.9
  3.7 11.5 %all_to_all.30.tiles = f32[2,512,384]{2,1,0:T(8,128)S(1)} all-to-all(f32[2,512,384]{2,1,0:T(8,128)S(1)} %bitcast.30), channel_id=1, replica_groups=mesh['zhi'=4,'zlo'=4,'core'=2,'lat'=16] {'core'}, dimensions={0} | all-to-all | bytes 3145728 | tf_op jit(solution)/shard_map/all_to_all | solution.py:26
  15.2 0.1 shard_map.68
  15.3 0.0 copy-start.3
  15.3 0.9 copy-done.3
  16.2 3.6 %all-to-all-start.1 = ((f32[4,128,384]{2,1,0:T(8,128)}), f32[4,128,384]{2,1,0:T(8,128)S(1)}, u32[]{:S(2)}, u32[]{:S(2)}) async-start(f32[4,128,384]{2,1,0:T(8,128)} %bitcast.23), calls=%async_computation.1 | async-start | bytes 1572864 | tf_op jit(solution)/shard_map/all_to_all | solution.py:26
  19.8 1.2 copy.7
  21.1 0.0 copy-start.6
  21.1 0.8 dynamic-slice_bitcast_fusion
  21.9 0.1 copy.10.bias
  22.0 0.0 copy-done.1
  22.0 1.3 copy.8
  23.3 16.3 %all-to-all-done.1.tiles = f32[4,128,384]{2,1,0:T(8,128)S(1)} async-done(((f32[4,128,384]{2,1,0:T(8,128)}), f32[4,128,384]{2,1,0:T(8,128)S(1)}, u32[]{:S(2)}, u32[]{:S(2)}) %all-to-all-start.1) | async-done | bytes 786464 | tf_op jit(solution)/shard_map/all_to_all | solution.py:26
  39.7 0.0 copy-start.2
  39.7 34.5 %all-gather = f32[512,384]{1,0:T(8,128)S(1)} all-gather(f32[128,384]{1,0:T(8,128)S(1)} %shard_map.69), channel_id=2, replica_groups=mesh['zhi'=4,'zlo'=4,'core'=2,'lat'=16] {'zhi'}, dimensions={0}, use_global_device_ids=true | all-gather | bytes 983040 | tf_op jit(solution)/shard_map/all_gather | solution.py:181
  74.2 0.1 shard_map.70
  74.3 17.7 %all_gather.23.right.acts = bf16[1024,384]{1,0:T(8,128)(2,1)S(1)} all-gather(bf16[128,384]{1,0:T(8,128)(2,1)S(1)} %get-tuple-element.10), channel_id=1, replica_groups=mesh['zhi'=4,'zlo'=4,'core'=2,'lat'=16] {'zlo','core'}, dimensions={0}, use_global_device_ids=true | all-gather | bytes 884736 | tf_op jit(solution)/shard_map/all_gather | solution.py:184
  92.0 0.0 copy-done.2
  92.0 0.7 shard_map.71
  92.7 0.0 copy-start.9
  92.8 0.7 copy-done.9
  93.5 6.4 %all-to-all-start.2 = ((bf16[16,32,384]{2,1,0:T(8,128)(2,1)}), bf16[16,32,384]{2,1,0:T(8,128)(2,1)}, u32[]{:S(2)}, u32[]{:S(2)}) async-start(bf16[16,32,384]{2,1,0:T(8,128)(2,1)} %bitcast.29), calls=%async_computation.2 | async-start | bytes 786432 | tf_op jit(solution)/shard_map/all_to_all | solution.py:26
  99.9 0.8 dynamic_slice.10
  100.6 0.0 copy-done.6
  100.6 0.1 convert_subtract_fusion.offset
  100.7 8.5 %all-to-all-done.2.tiles = bf16[16,32,384]{2,1,0:T(8,128)(2,1)} async-done(((bf16[16,32,384]{2,1,0:T(8,128)(2,1)}), bf16[16,32,384]{2,1,0:T(8,128)(2,1)}, u32[]{:S(2)}, u32[]{:S(2)}) %all-to-all-start.2) | async-done | bytes 393248 | tf_op jit(solution)/shard_map/all_to_all | solution.py:26
  109.2 1.1 shard_map.72
  110.3 11.6 %all_to_all.31 = bf16[16,32,384]{2,1,0:T(8,128)(2,1)S(1)} all-to-all(bf16[16,32,384]{2,1,0:T(8,128)(2,1)S(1)} %shard_map.72), channel_id=1, replica_groups=mesh['zhi'=4,'zlo'=4,'core'=2,'lat'=16] {'lat'}, dimensions={0} | all-to-all | bytes 786432 | tf_op jit(solution)/shard_map/all_to_all | solution.py:26
  121.9 0.7 shard_map.73
  122.6 6.6 %all_to_all.32.tiles = bf16[2,512,384]{2,1,0:T(8,128)(2,1)S(1)} all-to-all(bf16[2,512,384]{2,1,0:T(8,128)(2,1)S(1)} %bitcast.22), channel_id=1, replica_groups=mesh['zhi'=4,'zlo'=4,'core'=2,'lat'=16] {'core'}, dimensions={0} | all-to-all | bytes 1572864 | tf_op jit(solution)/shard_map/all_to_all | solution.py:26
  129.2 0.1 shard_map.74
  129.3 0.0 copy-start.8
  129.3 0.7 copy-done.8
  130.0 4.1 %all-to-all-start.5 = ((bf16[4,128,384]{2,1,0:T(8,128)(2,1)}), bf16[4,128,384]{2,1,0:T(8,128)(2,1)}, u32[]{:S(2)}, u32[]{:S(2)}) async-start(bf16[4,128,384]{2,1,0:T(8,128)(2,1)} %bitcast.28), calls=%async_computation.5 | async-start | bytes 786432 | tf_op jit(solution)/shard_map/all_to_all | solution.py:26
  134.2 1.2 shard_map.75
  135.4 0.0 copy-start.4
  135.4 1.3 copy-done.4
  136.8 8.9 %all-to-all-done.5.tiles = bf16[4,128,384]{2,1,0:T(8,128)(2,1)} async-done(((bf16[4,128,384]{2,1,0:T(8,128)(2,1)}), bf16[4,128,384]{2,1,0:T(8,128)(2,1)}, u32[]{:S(2)}, u32[]{:S(2)}) %all-to-all-start.5) | async-done | bytes 393248 | tf_op jit(solution)/shard_map/all_to_all | solution.py:26
  145.7 1.2 shard_map.76
  146.9 21.3 %all-gather.1 = bf16[576,384]{1,0:T(8,128)(2,1)S(1)} all-gather(bf16[144,384]{1,0:T(8,128)(2,1)S(1)} %shard_map.76), channel_id=3, replica_groups=mesh['zhi'=4,'zlo'=4,'core'=2,'lat'=16] {'zhi'}, dimensions={0}, use_global_device_ids=true | all-gather | bytes 552960 | tf_op jit(solution)/shard_map/all_gather | solution.py:209
  168.2 0.1 shard_map.77
  168.3 20.3 %all-gather.2 = bf16[1152,384]{1,0:T(8,128)(2,1)S(1)} all-gather(bf16[144,384]{1,0:T(8,128)(2,1)S(1)} %shard_map.77), channel_id=4, replica_groups=mesh['zhi'=4,'zlo'=4,'core'=2,'lat'=16] {'zlo','core'}, dimensions={0}, use_global_device_ids=true | all-gather | bytes 995328 | tf_op jit(solution)/shard_map/all_gather | solution.py:211
  188.6 0.0 copy-done.7
  188.6 0.0 copy-done.5
  188.6 2.1 %shard_map.78 = (bf16[512,1024]{1,0:T(8,128)(2,1)}, bf16[1024,512]{1,0:T(8,128)(2,1)}) custom-call(bf16[512,384]{1,0:T(8,128)(2,1)S(1)} %bitcast.27, bf16[8,144,384]{2,1,0:T(8,128)(2,1)S(1)} %bitcast.19, f32[1024,512]{1,0:T(8,128)S(1)} %copy-done.5, bf16[1024,512]{1,0:T(8,128)(2,1)S(1)} %copy-done.1), custom_call_target="tpu_custom_call" | custom-call | flops 402653184 | bytes 6520832 | tf_op jit(solution)/shard_map/pallas_call | solution.py:59
  (4 shorter events, 0.0 us)
Async XLA Ops:
  0.6 1.2 copy-start
  15.3 0.9 copy-start.3
  16.2 5.8 %copy-start.1 = (bf16[1024,512]{1,0:T(8,128)(2,1)S(1)}, bf16[1024,512]{1,0:T(8,128)(2,1)}, u32[]{:S(2)}) copy-start(bf16[1024,512]{1,0:T(8,128)(2,1)} %decoder.5) | copy-start | bytes 3145732
  16.2 23.5 %all-to-all-start.1 = ((f32[4,128,384]{2,1,0:T(8,128)}), f32[4,128,384]{2,1,0:T(8,128)S(1)}, u32[]{:S(2)}, u32[]{:S(2)}) async-start(f32[4,128,384]{2,1,0:T(8,128)} %bitcast.23), calls=%async_computation.1 | async-start | bytes 1572864 | tf_op jit(solution)/shard_map/all_to_all | solution.py:26
  21.1 79.6 %copy-start.6 = (bf16[384,512]{0,1:T(8,128)(2,1)}, bf16[384,512]{0,1:T(8,128)(2,1)S(1)}, u32[]{:S(2)}) copy-start(bf16[384,512]{0,1:T(8,128)(2,1)S(1)} %copy.7) | copy-start | bytes 1179652
  39.7 52.3 %copy-start.2 = (bf16[1024,512]{0,1:T(8,128)(2,1)S(1)}, bf16[1024,512]{0,1:T(8,128)(2,1)}, u32[]{:S(2)}) copy-start(bf16[1024,512]{0,1:T(8,128)(2,1)} %copy.8) | copy-start | bytes 3145732
  92.7 0.7 copy-start.9
  93.5 15.7 %all-to-all-start.2 = ((bf16[16,32,384]{2,1,0:T(8,128)(2,1)}), bf16[16,32,384]{2,1,0:T(8,128)(2,1)}, u32[]{:S(2)}, u32[]{:S(2)}) async-start(bf16[16,32,384]{2,1,0:T(8,128)(2,1)} %bitcast.29), calls=%async_computation.2 | async-start | bytes 786432 | tf_op jit(solution)/shard_map/all_to_all | solution.py:26
  129.3 0.7 copy-start.8
  130.0 15.6 %all-to-all-start.5 = ((bf16[4,128,384]{2,1,0:T(8,128)(2,1)}), bf16[4,128,384]{2,1,0:T(8,128)(2,1)}, u32[]{:S(2)}, u32[]{:S(2)}) async-start(bf16[4,128,384]{2,1,0:T(8,128)(2,1)} %bitcast.28), calls=%async_computation.5 | async-start | bytes 786432 | tf_op jit(solution)/shard_map/all_to_all | solution.py:26
  135.4 1.3 copy-start.4
  136.8 51.8 %copy-start.7 = (bf16[384,512]{0,1:T(8,128)(2,1)S(1)}, bf16[384,512]{0,1:T(8,128)(2,1)}, u32[]{:S(2)}) copy-start(bf16[384,512]{0,1:T(8,128)(2,1)} %copy-done.6) | copy-start | bytes 1179652
  145.7 42.9 %copy-start.5 = (f32[1024,512]{1,0:T(8,128)S(1)}, f32[1024,512]{1,0:T(8,128)}, u32[]{:S(2)}) copy-start(f32[1024,512]{1,0:T(8,128)} %copy-done.4) | copy-start | bytes 6291460

commit v5 on v4

--- a/solution.py
+++ b/solution.py
@@ -37,8 +37,8 @@
     out[...] = total(tiles).astype(out.dtype)
 
 
-def sum_of(tiles):
-    out = jax.ShapeDtypeStruct(tiles.shape[1:], tiles.dtype)
+def sum_of(tiles, kept):
+    out = jax.ShapeDtypeStruct(tiles.shape[1:], kept)
     return whole_in_vmem(total_body, [out], [tiles], tiles.size)[0]
 
 
@@ -71,10 +71,8 @@
     out[...] = dot(left[...], right[...], ((1,), (0,))).astype(out.dtype)
 
 
-def act_body(tiles, bias, act, active):
-    pre = total(tiles) + bias[...]
-    act[...] = jnp.maximum(pre, 0.0).astype(BF16)
-    active[...] = jnp.where(pre > 0.0, 1.0, 0.0)
+def act_body(tiles, bias, act):
+    act[...] = jnp.maximum(total(tiles) + bias[...], 0.0).astype(BF16)
 
 
 def error_body(tiles, offset, out):
@@ -83,13 +81,11 @@
         out[k] = error
 
 
-def dacts_body(decoder, error, out):
-    cores, zs, own = out.shape[:3]
-    for z in range(zs):
-        rows = decoder[z * cores * own : (z + 1) * cores * own, :]
-        part = dot(rows, error[...], ((1,), (0,))).astype(BF16)
-        for core in range(cores):
-            out[core, z] = part[core * own : (core + 1) * own, :]
+def dacts_body(kept, got, errors, out):
+    core = lax.axis_index("core")
+    part = dot(kept[...], errors[core], ((1,), (0,)))
+    part = part + dot(got[...], errors[1 - core], ((1,), (0,)))
+    out[...] = part.astype(BF16)
 
 
 def in_two(sums):
@@ -117,17 +113,31 @@
     stats[...] = in_two(sums[...])
 
 
-def joined_body(tiles, stats, out):
-    own = tiles.shape[1]
+def core_sum_body(tiles, exact, rounded):
+    pre = total(tiles)
+    rounded[...] = pre.astype(BF16)
+    far, near, own = exact.shape[:3]
+    for z in range(far):
+        for k in range(near):
+            at = (k * far + z) * own
+            exact[z, k] = pre[at : at + own, :]
+
+
+def joined_body(tiles, stats, pre, bias, out):
+    own, extra = tiles.shape[1], stats.shape[0]
     out[:own, :] = total(tiles).astype(BF16)
-    out[own:, :] = stats[...]
-
-
-def dpre_body(tiles, active, out):
-    own = active.shape[0]
-    sums = total(tiles)
-    dacts = sums[:own] + PENALTY
-    out[:own, :] = jnp.where(active[...] > 0.0, dacts, 0.0).astype(BF16)
+    out[own : own + extra, :] = stats[...]
+    out[own + extra :, :] = jnp.where(pre[...] + bias[...] > 0.0, 1.0, 0.0).astype(BF16)
+
+
+def dpre_body(tiles, out):
+    masked = tiles.shape[1] - out.shape[0]
+    own = tiles.shape[0] * masked
+    sums = total(tiles.at[:, : out.shape[0], :])
+    for k in range(tiles.shape[0]):
+        rows = slice(k * masked, (k + 1) * masked)
+        active = tiles[k, out.shape[0] :, :].astype(F32) > 0.0
+        out[rows, :] = jnp.where(active, sums[rows] + PENALTY, 0.0).astype(BF16)
     out[own:, :] = in_two(from_two(sums[own:]))
 
 
@@ -173,27 +183,54 @@
 
     partial = dot(encoder, residuals, ((0,), (1,))).reshape(zs, cores, own, tokens)
     partial = partial.transpose(1, 0, 2, 3).reshape(latents, tokens)
-    pre = sum_of(split_exchange(partial, "core"))
-    pre = sum_of(split_exchange(pre, "zlo"))
-    act, active = whole_in_vmem(
+    far = lax.axis_size("zhi")
+    exact, rounded = whole_in_vmem(
+        core_sum_body,
+        [shape((far, zs, own // far, tokens), F32), shape((zs * own, tokens), BF16)],
+        [split_exchange(partial, "core")],
+        latents * tokens,
+    )
+    near_bias = own_block(enc_bias, NEAR)
+    bias = near_bias[:, None]
+    own_bias = own_block(near_bias, "zhi")[:, None]
+    exact = lax.psum_scatter(
+        exact.reshape(zs * own, tokens), ("zhi", "zlo"), scatter_dimension=0, tiled=True
+    )
+    grouped = decoder.reshape(zs, cores, own, depth)
+    core = lax.axis_index("core")
+    kept, sent = (
+        lax.dynamic_index_in_dim(grouped, k, 1, False).reshape(zs * own, depth)
+        for k in (core, cores - 1 - core)
+    )
+    got = lax.ppermute(sent, "core", [(k, cores - 1 - k) for k in range(cores)])
+    offset = own_block(dec_bias, "lat")[:, None] - own_block(inputs, "lat").astype(F32)
+    rounded = sum_of(split_exchange(rounded, "zlo"), BF16)
+    rounded, offset, kept, got, bias, own_bias = lax.optimization_barrier(
+        (rounded, offset, kept, got, bias, own_bias)
+    )
+    (act,) = whole_in_vmem(
         act_body,
-        [shape(pre.shape, BF16), shape(pre.shape, F32)],
-        (lax.all_gather(pre, "zhi"), own_block(enc_bias, NEAR)[:, None]),
-        pre.size,
+        [shape(rounded.shape, BF16)],
+        (lax.all_gather(rounded, "zhi"), bias),
+        4 * rounded.size,
     )
     acts = lax.all_gather(act, NEAR, tiled=True)
 
     (recon,) = whole_in_vmem(product_body, [shape((depth, tokens), BF16)], (turned, acts), flops)
     tiles = split_exchange(recon, "lat")
-    offset = own_block(dec_bias, "lat")[:, None] - own_block(inputs, "lat").astype(F32)
     (copies,) = whole_in_vmem(
         error_body, [shape(tiles.shape, BF16)], (tiles, offset), tiles.size
     )
     error = exchange(copies, "lat").reshape(depth, tokens)
 
-    (partial,) = whole_in_vmem(
-        dacts_body, [shape((cores, zs, own, tokens), BF16)], (decoder, error), flops
-    )
+    error, exact = lax.optimization_barrier((error, exact))
+    (half,) = whole_in_vmem(
+        dacts_body,
+        [shape((zs * own, tokens), BF16)],
+        (kept, got, lax.all_gather(error, "core")),
+        flops,
+    )
+
     grad, stats = whole_in_vmem(
         grad_body,
         [shape((latents, depth), F32), shape((2 * latents // LANES, 3 * LANES), BF16)],
@@ -201,12 +238,14 @@
         flops,
         [pltpu.VMEM((latents // LANES, 3 * LANES), F32)],
     )
-    half = sum_of(exchange(partial.reshape(cores, zs * own, tokens), "core"))
     tiles = split_exchange(half, "zlo")
     both = shape((own + stats.shape[0], tokens), BF16)
-    (joined,) = whole_in_vmem(joined_body, [both], (tiles, stats), tiles.size)
+    everything = shape((both.shape[0] + own // far, tokens), BF16)
+    (joined,) = whole_in_vmem(
+        joined_body, [everything], (tiles, stats, exact, own_bias), tiles.size
+    )
     (dpre,) = whole_in_vmem(
-        dpre_body, [both], (lax.all_gather(joined, "zhi"), active), 4 * joined.size
+        dpre_body, [both], [lax.all_gather(joined, "zhi")], 4 * joined.size
     )
     carried = lax.all_gather(dpre, NEAR)
     enc_grad, new_decoder = whole_in_vmem(

time: 191 us -> 191 us (level)
  waiting for transfers between devices: 33.8 us -> 18.9 us
  between operations: 0.8 us -> 14.2 us
  local copies, waits for them, and re-layouts: 9.26 us -> 14 us
  blocking collectives: 124 us -> 120 us
    all_to_all x3, waiting for transfers between devices: 33.8 us -> 18.9 us  [exchange(): return lax.all_to_all(tiles, axis, split_axis=0, concat_axis=0, tiled=True)]
    all_gather x1 -> x2, blocking collectives: 34.5 us -> 27.4 us  [the longest x1 22.8 us: per_device(): lax.all_gather(rounded, 'zhi')]
    all_gather x1, blocking collectives: 17.7 us -> 21 us  [per_device(): acts = lax.all_gather(act, NEAR, tiled=True)]
    all_to_all x3, starting transfers between devices: 14.1 us -> 11.3 us  [exchange(): return lax.all_to_all(tiles, axis, split_axis=0, concat_axis=0, tiled=True)]
    all_to_all x3 -> x2, blocking collectives: 29.7 us -> 27.3 us  [exchange(): return lax.all_to_all(tiles, axis, split_axis=0, concat_axis=0, tiled=True)]
    ppermute x0 -> x1, starting transfers between devices: none -> 2.27 us  [per_device(): got = lax.ppermute(sent, 'core', [(k, cores - 1 - k) for k in range(cores)])]
    all_gather x1, blocking collectives: 21.3 us -> 23.5 us  [per_device(): lax.all_gather(joined, 'zhi')]
    unnamed x22 -> x30, local copies, waits for them, and re-layouts: 7.46 us -> 8.67 us
  transfers between devices with their start and end apart: 3 -> 5, of which waited for: 3 -> 3; matrix products, arithmetic and copies ran while one was open for 2% -> 4% of each run, Pallas kernels for 1% -> 1%
where the time goes in v5:
time: 191 us; the launch traced here: 190 us
  blocking collectives  120 us (63%)
  waiting for transfers between devices  18.9 us (10%)
  between operations  14.2 us (7%)
  local copies, waits for them, and re-layouts  14 us (7%)
  starting transfers between devices  13.6 us (7%)
  Pallas kernels  7.44 us (4%)
    all_to_all x2, blocking collectives, exchange(): return lax.all_to_all(tiles, axis, split_axis=0, concat_axis=0, tiled=True)  27.3 us
    all_gather x1, blocking collectives, per_device(): lax.all_gather(joined, 'zhi')  23.5 us
    all_gather x1, blocking collectives, per_device(): lax.all_gather(rounded, 'zhi')  22.8 us
    all_gather x1, blocking collectives, per_device(): acts = lax.all_gather(act, NEAR, tiled=True)  21 us
    all_gather x1, blocking collectives, per_device(): carried = lax.all_gather(dpre, NEAR)  20.6 us
    all_to_all x3, waiting for transfers between devices, exchange(): return lax.all_to_all(tiles, axis, split_axis=0, concat_axis=0, tiled=True)  18.9 us
    all_to_all x3, starting transfers between devices, exchange(): return lax.all_to_all(tiles, axis, split_axis=0, concat_axis=0, tiled=True)  11.3 us
    unnamed x30, local copies, waits for them, and re-layouts  8.67 us
  transfers between devices with their start and end apart: 5, of which 3 were waited for; matrix products, arithmetic and copies ran while one was open for 4% of the time, Pallas kernels for 1%

profile of v5, /device:TPU:1, one launch (start us, length us, event | category | flops | bytes accessed | tf_op | source)
XLA Modules:
  0.0 189.9 jit_solution(12766998757256415105)
XLA Ops:
  7.2 0.0 copy-start
  7.2 1.2 copy-done
  8.4 1.7 fusion
  10.1 0.1 copy.9
  10.3 11.5 %all_to_all.25.tiles = f32[2,512,384]{2,1,0:T(8,128)S(1)} all-to-all(f32[2,512,384]{2,1,0:T(8,128)S(1)} %bitcast.41), channel_id=1, replica_groups=mesh['zhi'=4,'zlo'=4,'core'=2,'lat'=16] {'core'}, dimensions={0} | all-to-all | bytes 3145728 | tf_op jit(solution)/shard_map/all_to_all | solution.py:26
  21.8 1.1 shard_map.68
  22.9 3.5 %all-to-all-start.1 = ((bf16[4,128,384]{2,1,0:T(8,128)(2,1)}), bf16[4,128,384]{2,1,0:T(8,128)(2,1)S(1)}, u32[]{:S(2)}, u32[]{:S(2)}) async-start(bf16[4,128,384]{2,1,0:T(8,128)(2,1)} %bitcast.5), calls=%async_computation.1 | async-start | bytes 786432 | tf_op jit(solution)/shard_map/all_to_all | solution.py:26
  26.3 0.0 reduce-scatter.2.cloned.1.call-start
  26.4 1.1 constant_dynamic-slice_fusion
  27.5 2.3 %collective-permute-start = (bf16[512,512]{1,0:T(8,128)(2,1)}, bf16[512,512]{1,0:T(8,128)(2,1)S(1)}, u32[]{:S(2)}, u32[]{:S(2)}) collective-permute-start(bf16[512,512]{1,0:T(8,128)(2,1)} %bitcast.8), channel_id=1, source_target_pairs={{0,16},{16,0},{1,17},{17,1},{2,18},{18,2},{3,19},{19,3},{4,20},{20... | collective-permute-start | bytes 1572872 | tf_op jit(solution)/shard_map/ppermute | solution.py:205
  29.8 0.0 reduce-scatter.2.cloned.1.call-update
  29.8 1.2 copy.7
  31.0 1.3 copy.8
  32.3 0.8 dynamic_slice.21
  33.1 1.3 dynamic-slice_bitcast_fusion.1
  34.4 1.3 dynamic-slice_bitcast_fusion
  35.7 0.1 convert_subtract_fusion.offset
  35.8 2.0 %all-to-all-done.1.tiles = bf16[4,128,384]{2,1,0:T(8,128)(2,1)S(1)} async-done(((bf16[4,128,384]{2,1,0:T(8,128)(2,1)}), bf16[4,128,384]{2,1,0:T(8,128)(2,1)S(1)}, u32[]{:S(2)}, u32[]{:S(2)}) %all-to-all-start.1) | async-done | bytes 393248 | tf_op jit(solution)/shard_map/all_to_all | solution.py:26
  37.7 0.1 shard_map.69
  37.8 0.0 collective-permute-done.got
  37.8 0.7 copy.12.bias
  38.5 22.8 %all-gather = bf16[512,384]{1,0:T(8,128)(2,1)S(1)} all-gather(bf16[128,384]{1,0:T(8,128)(2,1)S(1)} %shard_map.69), channel_id=2, replica_groups=mesh['zhi'=4,'zlo'=4,'core'=2,'lat'=16] {'zhi'}, dimensions={0}, use_global_device_ids=true | all-gather | bytes 491520 | tf_op jit(solution)/shard_map/all_gather | solution.py:214
  61.4 0.1 shard_map.70
  61.5 21.0 %all_gather.29.right.acts = bf16[1024,384]{1,0:T(8,128)(2,1)S(1)} all-gather(bf16[128,384]{1,0:T(8,128)(2,1)S(1)} %shard_map.70), channel_id=1, replica_groups=mesh['zhi'=4,'zlo'=4,'core'=2,'lat'=16] {'zlo','core'}, dimensions={0}, use_global_device_ids=true | all-gather | bytes 884736 | tf_op jit(solution)/shard_map/all_gather | solution.py:217
  82.5 0.7 shard_map.71
  83.2 15.8 %all_to_all.26.tiles = bf16[16,32,384]{2,1,0:T(8,128)(2,1)S(1)} all-to-all(bf16[16,32,384]{2,1,0:T(8,128)(2,1)S(1)} %bitcast.40), channel_id=1, replica_groups=mesh['zhi'=4,'zlo'=4,'core'=2,'lat'=16] {'lat'}, dimensions={0} | all-to-all | bytes 786432 | tf_op jit(solution)/shard_map/all_to_all | solution.py:26
  99.0 0.1 shard_map.72
  99.1 0.0 copy-start.8
  99.1 0.7 copy-done.8
  99.8 3.6 %all-to-all-start.3 = ((bf16[16,32,384]{2,1,0:T(8,128)(2,1)}), bf16[16,32,384]{2,1,0:T(8,128)(2,1)S(1)}, u32[]{:S(2)}, u32[]{:S(2)}) async-start(bf16[16,32,384]{2,1,0:T(8,128)(2,1)} %copy-done.8), calls=%async_computation.3 | async-start | bytes 786432 | tf_op jit(solution)/shard_map/all_to_all | solution.py:26
  103.5 0.0 reduce-scatter.2.cloned.1.call-done.pre
  103.5 8.1 %all-to-all-done.3 = bf16[16,32,384]{2,1,0:T(8,128)(2,1)S(1)} async-done(((bf16[16,32,384]{2,1,0:T(8,128)(2,1)}), bf16[16,32,384]{2,1,0:T(8,128)(2,1)S(1)}, u32[]{:S(2)}, u32[]{:S(2)}) %all-to-all-start.3) | async-done | bytes 393248 | tf_op jit(solution)/shard_map/all_to_all | solution.py:26
  111.6 4.6 %all-gather.1 = bf16[1024,384]{1,0:T(8,128)(2,1)S(1)} all-gather(bf16[512,384]{1,0:T(8,128)(2,1)S(1)} %bitcast.30), channel_id=3, replica_groups=mesh['zhi'=4,'zlo'=4,'core'=2,'lat'=16] {'core'}, dimensions={0}, use_global_device_ids=true | all-gather | bytes 1179648 | tf_op jit(solution)/shard_map/all_gather | solution.py:230
  116.2 1.0 copy-done.5
  117.3 1.0 copy-done.11
  118.3 0.7 shard_map.73
  119.0 0.0 copy-start.9
  119.0 0.7 copy-done.9
  119.8 4.2 %all-to-all-start.4 = ((bf16[4,128,384]{2,1,0:T(8,128)(2,1)}), bf16[4,128,384]{2,1,0:T(8,128)(2,1)}, u32[]{:S(2)}, u32[]{:S(2)}) async-start(bf16[4,128,384]{2,1,0:T(8,128)(2,1)} %bitcast.39), calls=%async_computation.5 | async-start | bytes 786432 | tf_op jit(solution)/shard_map/all_to_all | solution.py:26
  124.0 0.1 copy.13.bias
  124.1 1.2 shard_map.74
  125.4 1.3 copy-done.3
  126.7 8.8 %all-to-all-done.4.tiles = bf16[4,128,384]{2,1,0:T(8,128)(2,1)} async-done(((bf16[4,128,384]{2,1,0:T(8,128)(2,1)}), bf16[4,128,384]{2,1,0:T(8,128)(2,1)}, u32[]{:S(2)}, u32[]{:S(2)}) %all-to-all-start.4) | async-done | bytes 393248 | tf_op jit(solution)/shard_map/all_to_all | solution.py:26
  135.5 1.2 shard_map.75
  136.8 23.5 %all-gather.2 = bf16[704,384]{1,0:T(8,128)(2,1)S(1)} all-gather(bf16[176,384]{1,0:T(8,128)(2,1)S(1)} %shard_map.75), channel_id=4, replica_groups=mesh['zhi'=4,'zlo'=4,'core'=2,'lat'=16] {'zhi'}, dimensions={0}, use_global_device_ids=true | all-gather | bytes 675840 | tf_op jit(solution)/shard_map/all_gather | solution.py:248
  160.2 0.1 shard_map.76
  160.3 20.6 %all-gather.3 = bf16[1152,384]{1,0:T(8,128)(2,1)S(1)} all-gather(bf16[144,384]{1,0:T(8,128)(2,1)S(1)} %shard_map.76), channel_id=5, replica_groups=mesh['zhi'=4,'zlo'=4,'core'=2,'lat'=16] {'zlo','core'}, dimensions={0}, use_global_device_ids=true | all-gather | bytes 995328 | tf_op jit(solution)/shard_map/all_gather | solution.py:250
  180.9 2.1 %shard_map.77 = (bf16[512,1024]{1,0:T(8,128)(2,1)}, bf16[1024,512]{1,0:T(8,128)(2,1)}) custom-call(bf16[512,384]{1,0:T(8,128)(2,1)S(1)} %bitcast.37, bf16[8,144,384]{2,1,0:T(8,128)(2,1)S(1)} %bitcast.32, f32[1024,512]{1,0:T(8,128)S(1)} %copy-done.4, bf16[1024,512]{1,0:T(8,128)(2,1)S(1)} %copy-done.1), custom_call_target="tpu_custom_call" | custom-call | flops 402653184 | bytes 6520832 | tf_op jit(solution)/shard_map/pallas_call | solution.py:59
  (19 shorter events, 0.0 us)
Async XLA Ops:
  7.2 1.2 copy-start
  21.8 4.6 %copy-start.1 = (bf16[1024,512]{1,0:T(8,128)(2,1)S(1)}, bf16[1024,512]{1,0:T(8,128)(2,1)}, u32[]{:S(2)}) copy-start(bf16[1024,512]{1,0:T(8,128)(2,1)} %decoder.3) | copy-start | bytes 3145732
  22.9 14.9 %all-to-all-start.1 = ((bf16[4,128,384]{2,1,0:T(8,128)(2,1)}), bf16[4,128,384]{2,1,0:T(8,128)(2,1)S(1)}, u32[]{:S(2)}, u32[]{:S(2)}) async-start(bf16[4,128,384]{2,1,0:T(8,128)(2,1)} %bitcast.5), calls=%async_computation.1 | async-start | bytes 786432 | tf_op jit(solution)/shard_map/all_to_all | solution.py:26
  26.3 77.1 %reduce-scatter.2.cloned.1.call-start = ((), (), s32[]{:S(2)}) async-start(), calls=%async_computation.6 | async-start | bytes 835584 | tf_op jit(solution)/shard_map/reduce_scatter | solution.py:196
  27.5 10.3 %collective-permute-start = (bf16[512,512]{1,0:T(8,128)(2,1)}, bf16[512,512]{1,0:T(8,128)(2,1)S(1)}, u32[]{:S(2)}, u32[]{:S(2)}) collective-permute-start(bf16[512,512]{1,0:T(8,128)(2,1)} %bitcast.8), channel_id=1, source_target_pairs={{0,16},{16,0},{1,17},{17,1},{2,18},{18,2},{3,19},{19,3},{4,20},{20... | collective-permute-start | bytes 1572872 | tf_op jit(solution)/shard_map/ppermute | solution.py:205
  31.0 30.3 %copy-start.6 = (bf16[384,512]{0,1:T(8,128)(2,1)}, bf16[384,512]{0,1:T(8,128)(2,1)S(1)}, u32[]{:S(2)}) copy-start(bf16[384,512]{0,1:T(8,128)(2,1)S(1)} %copy.7) | copy-start | bytes 1179652
  37.8 45.4 %copy-start.10 = (bf16[512,512]{1,0:T(8,128)(2,1)}, bf16[512,512]{1,0:T(8,128)(2,1)S(1)}, u32[]{:S(2)}) copy-start(bf16[512,512]{1,0:T(8,128)(2,1)S(1)} %collective-permute-done.got) | copy-start | bytes 1572868
  38.5 43.9 %copy-start.2 = (bf16[1024,512]{0,1:T(8,128)(2,1)S(1)}, bf16[1024,512]{0,1:T(8,128)(2,1)}, u32[]{:S(2)}) copy-start(bf16[1024,512]{0,1:T(8,128)(2,1)} %copy.8) | copy-start | bytes 3145732
  99.1 0.7 copy-start.8
  99.8 11.8 %all-to-all-start.3 = ((bf16[16,32,384]{2,1,0:T(8,128)(2,1)}), bf16[16,32,384]{2,1,0:T(8,128)(2,1)S(1)}, u32[]{:S(2)}, u32[]{:S(2)}) async-start(bf16[16,32,384]{2,1,0:T(8,128)(2,1)} %copy-done.8), calls=%async_computation.3 | async-start | bytes 786432 | tf_op jit(solution)/shard_map/all_to_all | solution.py:26
  116.2 7.8 %copy-start.13 = (f32[32,1]{0,1:T(1,128)S(1)}, f32[32,1]{0,1:T(1,128)}, u32[]{:S(2)}) copy-start(f32[32,1]{0,1:T(1,128)} %dynamic-slice_bitcast_fusion) | copy-start | bytes 388
  116.2 1.0 copy-start.5
  117.3 1.0 copy-start.11
  119.0 0.7 copy-start.9
  119.8 15.7 %copy-start.12 = (f32[32,384]{1,0:T(8,128)S(1)}, f32[32,384]{1,0:T(8,128)}, u32[]{:S(2)}) copy-start(f32[32,384]{1,0:T(8,128)} %reduce-scatter.2.cloned.1.call-done.pre) | copy-start | bytes 147460
  119.8 15.7 %all-to-all-start.4 = ((bf16[4,128,384]{2,1,0:T(8,128)(2,1)}), bf16[4,128,384]{2,1,0:T(8,128)(2,1)}, u32[]{:S(2)}, u32[]{:S(2)}) async-start(bf16[4,128,384]{2,1,0:T(8,128)(2,1)} %bitcast.39), calls=%async_computation.5 | async-start | bytes 786432 | tf_op jit(solution)/shard_map/all_to_all | solution.py:26
  125.4 1.3 copy-start.3
  126.7 54.2 %copy-start.7 = (bf16[384,512]{0,1:T(8,128)(2,1)S(1)}, bf16[384,512]{0,1:T(8,128)(2,1)}, u32[]{:S(2)}) copy-start(bf16[384,512]{0,1:T(8,128)(2,1)} %copy-done.6) | copy-start | bytes 1179652
  135.5 45.4 %copy-start.4 = (f32[1024,512]{1,0:T(8,128)S(1)}, f32[1024,512]{1,0:T(8,128)}, u32[]{:S(2)}) copy-start(f32[1024,512]{1,0:T(8,128)} %copy-done.3) | copy-start | bytes 6291460
Sparse Core Ops, SparseCore 0:
  30.6 62.4 reduce-scatter.1

commit v6 on v5

--- a/solution.py
+++ b/solution.py
@@ -205,9 +205,7 @@
     got = lax.ppermute(sent, "core", [(k, cores - 1 - k) for k in range(cores)])
     offset = own_block(dec_bias, "lat")[:, None] - own_block(inputs, "lat").astype(F32)
     rounded = sum_of(split_exchange(rounded, "zlo"), BF16)
-    rounded, offset, kept, got, bias, own_bias = lax.optimization_barrier(
-        (rounded, offset, kept, got, bias, own_bias)
-    )
+    rounded, offset, kept, got = lax.optimization_barrier((rounded, offset, kept, got))
     (act,) = whole_in_vmem(
         act_body,
         [shape(rounded.shape, BF16)],
@@ -223,7 +221,6 @@
     )
     error = exchange(copies, "lat").reshape(depth, tokens)
 
-    error, exact = lax.optimization_barrier((error, exact))
     (half,) = whole_in_vmem(
         dacts_body,
         [shape((zs * own, tokens), BF16)],
@@ -238,6 +235,7 @@
         flops,
         [pltpu.VMEM((latents // LANES, 3 * LANES), F32)],
     )
+    half, exact = lax.optimization_barrier((half, exact))
     tiles = split_exchange(half, "zlo")
     both = shape((own + stats.shape[0], tokens), BF16)
     everything = shape((both.shape[0] + own // far, tokens), BF16)

time: 191 us -> 186 us (0.974)
  blocking collectives: 120 us -> 130 us
  waiting for transfers between devices: 18.9 us -> 11.8 us
  local copies, waits for them, and re-layouts: 14 us -> 9.49 us
  starting transfers between devices: 13.6 us -> 10 us
    all_to_all x2 -> x3, blocking collectives: 27.3 us -> 39.1 us  [exchange(): return lax.all_to_all(tiles, axis, split_axis=0, concat_axis=0, tiled=True)]
    all_to_all x3 -> x2, waiting for transfers between devices: 18.9 us -> 11.8 us  [exchange(): return lax.all_to_all(tiles, axis, split_axis=0, concat_axis=0, tiled=True)]
    all_gather x1, blocking collectives: 20.6 us -> 16.7 us  [per_device(): carried = lax.all_gather(dpre, NEAR)]
    all_to_all x3 -> x2, starting transfers between devices: 11.3 us -> 7.7 us  [exchange(): return lax.all_to_all(tiles, axis, split_axis=0, concat_axis=0, tiled=True)]
    all_gather x1, blocking collectives: 23.5 us -> 26.8 us  [per_device(): lax.all_gather(joined, 'zhi')]
    unnamed x30 -> x26, local copies, waits for them, and re-layouts: 8.67 us -> 5.85 us
  transfers between devices with their start and end apart: 5 -> 4, of which waited for: 3 -> 2; matrix products, arithmetic and copies ran while one was open for 4% -> 3% of each run, Pallas kernels for 1% -> 2%
where the time goes in v6:
time: 186 us; the launch traced here: 185 us
  blocking collectives  130 us (70%)
  between operations  14.2 us (8%)
  waiting for transfers between devices  11.8 us (6%)
  starting transfers between devices  10 us (5%)
  local copies, waits for them, and re-layouts  9.49 us (5%)
  Pallas kernels  7.43 us (4%)
    all_to_all x3, blocking collectives, exchange(): return lax.all_to_all(tiles, axis, split_axis=0, concat_axis=0, tiled=True)  39.1 us
    all_gather x1, blocking collectives, per_device(): lax.all_gather(joined, 'zhi')  26.8 us
    all_gather x1, blocking collectives, per_device(): lax.all_gather(rounded, 'zhi')  23.4 us
    all_gather x1, blocking collectives, per_device(): acts = lax.all_gather(act, NEAR, tiled=True)  19.6 us
    all_gather x1, blocking collectives, per_device(): carried = lax.all_gather(dpre, NEAR)  16.7 us
    all_to_all x2, waiting for transfers between devices, exchange(): return lax.all_to_all(tiles, axis, split_axis=0, concat_axis=0, tiled=True)  11.8 us
    all_to_all x2, starting transfers between devices, exchange(): return lax.all_to_all(tiles, axis, split_axis=0, concat_axis=0, tiled=True)  7.7 us
    pallas_call x10, Pallas kernels, whole_in_vmem(): pl.pallas_call(body, out_shape=outs, in_specs=[spec] * len(operands), out...  7.43 us
  transfers between devices with their start and end apart: 4, of which 2 were waited for; matrix products, arithmetic and copies ran while one was open for 3% of the time, Pallas kernels for 2%

profile of v6, /device:TPU:1, one launch (start us, length us, event | category | flops | bytes accessed | tf_op | source)
XLA Modules:
  0.0 185.0 jit_solution(4517179769317162203)
XLA Ops:
  7.2 0.0 copy-start
  7.2 1.2 copy-done
  8.4 1.7 fusion
  10.1 0.1 copy.16
  10.3 11.5 %all_to_all.25.tiles = f32[2,512,384]{2,1,0:T(8,128)S(1)} all-to-all(f32[2,512,384]{2,1,0:T(8,128)S(1)} %bitcast.40), channel_id=1, replica_groups=mesh['zhi'=4,'zlo'=4,'core'=2,'lat'=16] {'core'}, dimensions={0} | all-to-all | bytes 3145728 | tf_op jit(solution)/shard_map/all_to_all | solution.py:26
  21.8 1.1 shard_map.68
  22.9 3.5 %all-to-all-start.1 = ((bf16[4,128,384]{2,1,0:T(8,128)(2,1)}), bf16[4,128,384]{2,1,0:T(8,128)(2,1)S(1)}, u32[]{:S(2)}, u32[]{:S(2)}) async-start(bf16[4,128,384]{2,1,0:T(8,128)(2,1)} %bitcast.5), calls=%async_computation.1 | async-start | bytes 786432 | tf_op jit(solution)/shard_map/all_to_all | solution.py:26
  26.4 0.0 reduce-scatter.2.cloned.1.call-start
  26.4 0.0 copy-done.1
  26.4 1.0 constant_dynamic-slice_fusion
  27.5 2.3 %collective-permute-start = (bf16[512,512]{1,0:T(8,128)(2,1)}, bf16[512,512]{1,0:T(8,128)(2,1)S(1)}, u32[]{:S(2)}, u32[]{:S(2)}) collective-permute-start(bf16[512,512]{1,0:T(8,128)(2,1)} %bitcast.8), channel_id=1, source_target_pairs={{0,16},{16,0},{1,17},{17,1},{2,18},{18,2},{3,19},{19,3},{4,20},{20... | collective-permute-start | bytes 1572872 | tf_op jit(solution)/shard_map/ppermute | solution.py:205
  29.7 0.0 reduce-scatter.2.cloned.1.call-update
  29.8 1.2 copy.14
  31.0 0.0 copy-start.6
  31.0 1.3 copy.15
  32.3 0.8 dynamic_slice.21
  33.1 0.1 convert_subtract_fusion.offset
  33.1 0.8 dynamic-slice_bitcast_fusion.1
  33.9 0.1 copy.19.bias
  34.0 3.7 %all-to-all-done.1.tiles = bf16[4,128,384]{2,1,0:T(8,128)(2,1)S(1)} async-done(((bf16[4,128,384]{2,1,0:T(8,128)(2,1)}), bf16[4,128,384]{2,1,0:T(8,128)(2,1)S(1)}, u32[]{:S(2)}, u32[]{:S(2)}) %all-to-all-start.1) | async-done | bytes 393248 | tf_op jit(solution)/shard_map/all_to_all | solution.py:26
  37.8 0.1 shard_map.69
  37.8 0.0 collective-permute-done.got
  37.8 0.0 copy-start.9
  37.8 23.4 %all-gather = bf16[512,384]{1,0:T(8,128)(2,1)S(1)} all-gather(bf16[128,384]{1,0:T(8,128)(2,1)S(1)} %shard_map.69), channel_id=2, replica_groups=mesh['zhi'=4,'zlo'=4,'core'=2,'lat'=16] {'zhi'}, dimensions={0}, use_global_device_ids=true | all-gather | bytes 491520 | tf_op jit(solution)/shard_map/all_gather | solution.py:212
  61.2 0.0 copy-done.6
  61.2 0.1 shard_map.70
  61.3 19.6 %all_gather.26.right.acts = bf16[1024,384]{1,0:T(8,128)(2,1)S(1)} all-gather(bf16[128,384]{1,0:T(8,128)(2,1)S(1)} %shard_map.70), channel_id=1, replica_groups=mesh['zhi'=4,'zlo'=4,'core'=2,'lat'=16] {'zlo','core'}, dimensions={0}, use_global_device_ids=true | all-gather | bytes 884736 | tf_op jit(solution)/shard_map/all_gather | solution.py:215
  80.9 0.7 shard_map.71
  81.7 0.0 copy-done.9
  81.7 15.9 %all_to_all.26.tiles = bf16[16,32,384]{2,1,0:T(8,128)(2,1)S(1)} all-to-all(bf16[16,32,384]{2,1,0:T(8,128)(2,1)S(1)} %bitcast.39), channel_id=1, replica_groups=mesh['zhi'=4,'zlo'=4,'core'=2,'lat'=16] {'lat'}, dimensions={0} | all-to-all | bytes 786432 | tf_op jit(solution)/shard_map/all_to_all | solution.py:26
  97.6 0.1 shard_map.72
  97.7 11.7 %all_to_all.27 = bf16[16,32,384]{2,1,0:T(8,128)(2,1)S(1)} all-to-all(bf16[16,32,384]{2,1,0:T(8,128)(2,1)S(1)} %shard_map.72), channel_id=1, replica_groups=mesh['zhi'=4,'zlo'=4,'core'=2,'lat'=16] {'lat'}, dimensions={0} | all-to-all | bytes 786432 | tf_op jit(solution)/shard_map/all_to_all | solution.py:26
  109.4 4.6 %all_gather.27.errors = bf16[2,512,384]{2,1,0:T(8,128)(2,1)S(1)} all-gather(bf16[1,512,384]{2,1,0:T(8,128)(2,1)S(1)} %bitcast.30), channel_id=1, replica_groups=mesh['zhi'=4,'zlo'=4,'core'=2,'lat'=16] {'core'}, dimensions={0}, use_global_device_ids=true | all-gather | bytes 1179648 | tf_op jit(solution)/shard_map/all_gather | solution.py:227
  114.0 0.7 shard_map.73
  114.7 0.0 copy-start.8
  114.7 0.7 copy-done.8
  115.5 4.2 %all-to-all-start.4 = ((bf16[4,128,384]{2,1,0:T(8,128)(2,1)}), bf16[4,128,384]{2,1,0:T(8,128)(2,1)}, u32[]{:S(2)}, u32[]{:S(2)}) async-start(bf16[4,128,384]{2,1,0:T(8,128)(2,1)} %bitcast.38), calls=%async_computation.5 | async-start | bytes 786432 | tf_op jit(solution)/shard_map/all_to_all | solution.py:26
  119.7 0.8 dynamic-slice_bitcast_fusion
  120.5 0.1 copy.20.bias
  120.6 1.2 shard_map.74
  121.8 0.0 copy-start.3
  121.8 1.3 copy-done.3
  123.2 8.0 %all-to-all-done.4.tiles = bf16[4,128,384]{2,1,0:T(8,128)(2,1)} async-done(((bf16[4,128,384]{2,1,0:T(8,128)(2,1)}), bf16[4,128,384]{2,1,0:T(8,128)(2,1)}, u32[]{:S(2)}, u32[]{:S(2)}) %all-to-all-start.4) | async-done | bytes 393248 | tf_op jit(solution)/shard_map/all_to_all | solution.py:26
  131.2 1.2 shard_map.75
  132.5 26.8 %all-gather.1 = bf16[704,384]{1,0:T(8,128)(2,1)S(1)} all-gather(bf16[176,384]{1,0:T(8,128)(2,1)S(1)} %shard_map.75), channel_id=3, replica_groups=mesh['zhi'=4,'zlo'=4,'core'=2,'lat'=16] {'zhi'}, dimensions={0}, use_global_device_ids=true | all-gather | bytes 675840 | tf_op jit(solution)/shard_map/all_gather | solution.py:246
  159.3 0.1 shard_map.76
  159.3 16.7 %all-gather.2 = bf16[1152,384]{1,0:T(8,128)(2,1)S(1)} all-gather(bf16[144,384]{1,0:T(8,128)(2,1)S(1)} %shard_map.76), channel_id=4, replica_groups=mesh['zhi'=4,'zlo'=4,'core'=2,'lat'=16] {'zlo','core'}, dimensions={0}, use_global_device_ids=true | all-gather | bytes 995328 | tf_op jit(solution)/shard_map/all_gather | solution.py:248
  176.1 2.1 %shard_map.77 = (bf16[512,1024]{1,0:T(8,128)(2,1)}, bf16[1024,512]{1,0:T(8,128)(2,1)}) custom-call(bf16[512,384]{1,0:T(8,128)(2,1)S(1)} %bitcast.36, bf16[8,144,384]{2,1,0:T(8,128)(2,1)S(1)} %bitcast.32, f32[1024,512]{1,0:T(8,128)S(1)} %copy-done.4, bf16[1024,512]{1,0:T(8,128)(2,1)S(1)} %copy-done.1), custom_call_target="tpu_custom_call" | custom-call | flops 402653184 | bytes 6520832 | tf_op jit(solution)/shard_map/pallas_call | solution.py:59
  (14 shorter events, 0.0 us)
Async XLA Ops:
  7.2 1.2 copy-start
  21.8 4.6 %copy-start.1 = (bf16[1024,512]{1,0:T(8,128)(2,1)S(1)}, bf16[1024,512]{1,0:T(8,128)(2,1)}, u32[]{:S(2)}) copy-start(bf16[1024,512]{1,0:T(8,128)(2,1)} %decoder.3) | copy-start | bytes 3145732
  22.9 14.9 %all-to-all-start.1 = ((bf16[4,128,384]{2,1,0:T(8,128)(2,1)}), bf16[4,128,384]{2,1,0:T(8,128)(2,1)S(1)}, u32[]{:S(2)}, u32[]{:S(2)}) async-start(bf16[4,128,384]{2,1,0:T(8,128)(2,1)} %bitcast.5), calls=%async_computation.1 | async-start | bytes 786432 | tf_op jit(solution)/shard_map/all_to_all | solution.py:26
  26.4 89.1 %reduce-scatter.2.cloned.1.call-start = ((), (), s32[]{:S(2)}) async-start(), calls=%async_computation.6 | async-start | bytes 835584 | tf_op jit(solution)/shard_map/reduce_scatter | solution.py:196
  27.5 10.3 %collective-permute-start = (bf16[512,512]{1,0:T(8,128)(2,1)}, bf16[512,512]{1,0:T(8,128)(2,1)S(1)}, u32[]{:S(2)}, u32[]{:S(2)}) collective-permute-start(bf16[512,512]{1,0:T(8,128)(2,1)} %bitcast.8), channel_id=1, source_target_pairs={{0,16},{16,0},{1,17},{17,1},{2,18},{18,2},{3,19},{19,3},{4,20},{20... | collective-permute-start | bytes 1572872 | tf_op jit(solution)/shard_map/ppermute | solution.py:205
  31.0 30.3 %copy-start.6 = (bf16[384,512]{0,1:T(8,128)(2,1)}, bf16[384,512]{0,1:T(8,128)(2,1)S(1)}, u32[]{:S(2)}) copy-start(bf16[384,512]{0,1:T(8,128)(2,1)S(1)} %copy.14) | copy-start | bytes 1179652
  37.8 43.2 %copy-start.2 = (bf16[1024,512]{0,1:T(8,128)(2,1)S(1)}, bf16[1024,512]{0,1:T(8,128)(2,1)}, u32[]{:S(2)}) copy-start(bf16[1024,512]{0,1:T(8,128)(2,1)} %copy.15) | copy-start | bytes 3145732
  37.8 43.8 %copy-start.9 = (bf16[512,512]{1,0:T(8,128)(2,1)}, bf16[512,512]{1,0:T(8,128)(2,1)S(1)}, u32[]{:S(2)}) copy-start(bf16[512,512]{1,0:T(8,128)(2,1)S(1)} %collective-permute-done.got) | copy-start | bytes 1572868
  97.6 16.4 %copy-start.5 = (bf16[4,1,128,512]{3,2,1,0:T(8,128)(2,1)S(1)}, bf16[4,1,128,512]{3,2,1,0:T(8,128)(2,1)}, u32[]{:S(2)}) copy-start(bf16[4,1,128,512]{3,2,1,0:T(8,128)(2,1)} %get-tuple-element.27) | copy-start | bytes 1572868
  97.6 16.4 %copy-start.10 = (bf16[512,512]{1,0:T(8,128)(2,1)S(1)}, bf16[512,512]{1,0:T(8,128)(2,1)}, u32[]{:S(2)}) copy-start(bf16[512,512]{1,0:T(8,128)(2,1)} %copy-done.9) | copy-start | bytes 1572868
  114.7 0.7 copy-start.8
  115.5 15.7 %copy-start.11 = (f32[32,384]{1,0:T(8,128)S(1)}, f32[32,384]{1,0:T(8,128)}, u32[]{:S(2)}) copy-start(f32[32,384]{1,0:T(8,128)} %reduce-scatter.2.cloned.1.call-done.pre) | copy-start | bytes 147460
  115.5 15.7 %all-to-all-start.4 = ((bf16[4,128,384]{2,1,0:T(8,128)(2,1)}), bf16[4,128,384]{2,1,0:T(8,128)(2,1)}, u32[]{:S(2)}, u32[]{:S(2)}) async-start(bf16[4,128,384]{2,1,0:T(8,128)(2,1)} %bitcast.38), calls=%async_computation.5 | async-start | bytes 786432 | tf_op jit(solution)/shard_map/all_to_all | solution.py:26
  121.8 1.3 copy-start.3
  123.2 52.9 %copy-start.7 = (bf16[384,512]{0,1:T(8,128)(2,1)S(1)}, bf16[384,512]{0,1:T(8,128)(2,1)}, u32[]{:S(2)}) copy-start(bf16[384,512]{0,1:T(8,128)(2,1)} %copy-done.6) | copy-start | bytes 1179652
  131.2 44.9 %copy-start.4 = (f32[1024,512]{1,0:T(8,128)S(1)}, f32[1024,512]{1,0:T(8,128)}, u32[]{:S(2)}) copy-start(f32[1024,512]{1,0:T(8,128)} %copy-done.3) | copy-start | bytes 6291460
Sparse Core Ops, SparseCore 0:
  30.6 61.9 reduce-scatter.1

commit v7 on v6

--- a/solution.py
+++ b/solution.py
@@ -65,6 +65,25 @@
         compiler_params=pltpu.CompilerParams(vmem_limit_bytes=16 * 2**20),
         cost_estimate=pl.CostEstimate(flops=flops, bytes_accessed=size, transcendentals=0),
     )(*operands)
+
+
+def pre_body(encoder, residuals, out, held, tokens, arrived, ready):
+    cores, zs, own = out.shape[:3]
+    wide = cores * own
+    first = pltpu.make_async_copy(residuals, tokens, ready)
+    first.start()
+    copies = []
+    for z in range(zs):
+        at = (slice(None), pl.ds(z * wide, wide))
+        copies.append(pltpu.make_async_copy(encoder.at[at], held.at[at], arrived.at[z]))
+        copies[z].start()
+    first.wait()
+    for z in range(zs):
+        copies[z].wait()
+        columns = held[:, z * wide : (z + 1) * wide]
+        part = dot(columns, tokens[...], ((0,), (1,)))
+        for core in range(cores):
+            out[core, z] = part[core * own : (core + 1) * own, :]
 
 
 def product_body(left, right, out):
@@ -181,8 +200,23 @@
     shape = jax.ShapeDtypeStruct
     inputs, turned = lax.optimization_barrier((residuals.T, decoder.T))
 
-    partial = dot(encoder, residuals, ((0,), (1,))).reshape(zs, cores, own, tokens)
-    partial = partial.transpose(1, 0, 2, 3).reshape(latents, tokens)
+    spec = pl.BlockSpec(memory_space=pltpu.HBM)
+    partial = pl.pallas_call(
+        pre_body,
+        out_shape=shape((cores, zs, own, tokens), F32),
+        in_specs=[spec, spec],
+        out_specs=pl.BlockSpec(memory_space=pltpu.VMEM),
+        scratch_shapes=[
+            pltpu.VMEM(encoder.shape, BF16),
+            pltpu.VMEM(residuals.shape, BF16),
+            pltpu.SemaphoreType.DMA((zs,)),
+            pltpu.SemaphoreType.DMA,
+        ],
+        compiler_params=pltpu.CompilerParams(vmem_limit_bytes=61 * 2**20),
+        cost_estimate=pl.CostEstimate(
+            flops=flops, bytes_accessed=2 * encoder.size, transcendentals=0
+        ),
+    )(encoder, residuals).reshape(latents, tokens)
     far = lax.axis_size("zhi")
     exact, rounded = whole_in_vmem(
         core_sum_body,

time: 186 us -> 186 us (level)
  local copies, waits for them, and re-layouts: 9.49 us -> 4.28 us
  Pallas kernels: 7.43 us -> 11.9 us
  waiting for transfers between devices: 11.8 us -> 14.8 us
    pallas_call x0 -> x1, Pallas kernels: none -> 3.83 us  [per_device(): pl.pallas_call(pre_body, out_shape=shape((cores, zs, own, tokens), F32),...]
    unnamed x26 -> x20, local copies, waits for them, and re-layouts: 5.85 us -> 2.12 us
    all_gather x1, blocking collectives: 16.7 us -> 20.1 us  [per_device(): carried = lax.all_gather(dpre, NEAR)]
    all_gather x1, blocking collectives: 26.8 us -> 23.5 us  [per_device(): lax.all_gather(joined, 'zhi')]
    all_to_all x2, waiting for transfers between devices: 11.8 us -> 14.7 us  [exchange(): return lax.all_to_all(tiles, axis, split_axis=0, concat_axis=0, tiled=True)]
  transfers between devices with their start and end apart: 4 -> 4, of which waited for: 2 -> 2; matrix products, arithmetic and copies ran while one was open for 3% -> 2% of each run, Pallas kernels for 2% -> 3%
where the time goes in v7:
time: 186 us
  blocking collectives  131 us (70%)
  waiting for transfers between devices  14.8 us (8%)
  between operations  14.2 us (8%)
  Pallas kernels  11.9 us (6%)
  starting transfers between devices  9.36 us (5%)
  local copies, waits for them, and re-layouts  4.28 us (2%)
    all_to_all x3, blocking collectives, exchange(): return lax.all_to_all(tiles, axis, split_axis=0, concat_axis=0, tiled=True)  40.1 us
    all_gather x1, blocking collectives, per_device(): lax.all_gather(rounded, 'zhi')  24.7 us
    all_gather x1, blocking collectives, per_device(): lax.all_gather(joined, 'zhi')  23.5 us
    all_gather x1, blocking collectives, per_device(): carried = lax.all_gather(dpre, NEAR)  20.1 us
    all_gather x1, blocking collectives, per_device(): acts = lax.all_gather(act, NEAR, tiled=True)  18.3 us
    all_to_all x2, waiting for transfers between devices, exchange(): return lax.all_to_all(tiles, axis, split_axis=0, concat_axis=0, tiled=True)  14.7 us
    pallas_call x10, Pallas kernels, whole_in_vmem(): pl.pallas_call(body, out_shape=outs, in_specs=[spec] * len(operands), out...  8.11 us
    all_to_all x2, starting transfers between devices, exchange(): return lax.all_to_all(tiles, axis, split_axis=0, concat_axis=0, tiled=True)  7.05 us
  transfers between devices with their start and end apart: 4, of which 2 were waited for; matrix products, arithmetic and copies ran while one was open for 2% of the time, Pallas kernels for 3%

profile of v7, /device:TPU:1, one launch (start us, length us, event | category | flops | bytes accessed | tf_op | source)
XLA Modules:
  0.0 185.9 jit_solution(11968618517464278390)
XLA Ops:
  7.2 0.0 copy-start
  7.2 3.8 %shard_map.68 = f32[2,4,128,384]{3,2,1,0:T(8,128)} custom-call(bf16[512,1024]{1,0:T(8,128)(2,1)} %encoder.1, bf16[384,512]{1,0:T(8,128)(2,1)} %residuals.1), custom_call_target="tpu_custom_call" | custom-call | flops 402653184 | bytes 1048576 | tf_op jit(solution)/shard_map/pallas_call | solution.py:204
  11.0 12.7 %all_to_all.25.tiles = f32[2,512,384]{2,1,0:T(8,128)S(1)} all-to-all(f32[2,512,384]{2,1,0:T(8,128)} %bitcast.34), channel_id=1, replica_groups=mesh['zhi'=4,'zlo'=4,'core'=2,'lat'=16] {'core'}, dimensions={0} | all-to-all | bytes 3145728 | tf_op jit(solution)/shard_map/all_to_all | solution.py:26
  23.7 1.1 shard_map.69
  24.8 3.5 %all-to-all-start.1 = ((bf16[4,128,384]{2,1,0:T(8,128)(2,1)}), bf16[4,128,384]{2,1,0:T(8,128)(2,1)S(1)}, u32[]{:S(2)}, u32[]{:S(2)}) async-start(bf16[4,128,384]{2,1,0:T(8,128)(2,1)} %bitcast.3), calls=%async_computation.1 | async-start | bytes 786432 | tf_op jit(solution)/shard_map/all_to_all | solution.py:26
  28.3 0.0 copy-start.8
  28.3 0.0 reduce-scatter.2.cloned.1.call-start
  28.3 0.0 copy-done.1
  28.4 1.0 constant_dynamic-slice_fusion
  29.4 2.3 %collective-permute-start = (bf16[512,512]{1,0:T(8,128)(2,1)}, bf16[512,512]{1,0:T(8,128)(2,1)}, u32[]{:S(2)}, u32[]{:S(2)}) collective-permute-start(bf16[512,512]{1,0:T(8,128)(2,1)} %bitcast.6), channel_id=1, source_target_pairs={{0,16},{16,0},{1,17},{17,1},{2,18},{18,2},{3,19},{19,3},{4,20},{20... | collective-permute-start | bytes 1572872 | tf_op jit(solution)/shard_map/ppermute | solution.py:239
  31.7 0.0 reduce-scatter.2.cloned.1.call-update
  31.7 0.0 copy-done.8
  31.7 0.2 copy.13
  31.9 0.0 copy-start.5
  31.9 0.5 copy.14
  32.5 0.8 dynamic_slice.21
  33.2 0.1 convert_subtract_fusion.offset
  33.3 0.0 copy-done
  33.3 0.1 dynamic-slice_bitcast_fusion.1
  33.4 0.1 copy.17.bias
  33.5 6.2 %all-to-all-done.1.tiles = bf16[4,128,384]{2,1,0:T(8,128)(2,1)S(1)} async-done(((bf16[4,128,384]{2,1,0:T(8,128)(2,1)}), bf16[4,128,384]{2,1,0:T(8,128)(2,1)S(1)}, u32[]{:S(2)}, u32[]{:S(2)}) %all-to-all-start.1) | async-done | bytes 393248 | tf_op jit(solution)/shard_map/all_to_all | solution.py:26
  39.7 0.1 shard_map.70
  39.7 0.0 collective-permute-done.got
  39.7 24.7 %all-gather = bf16[512,384]{1,0:T(8,128)(2,1)S(1)} all-gather(bf16[128,384]{1,0:T(8,128)(2,1)S(1)} %shard_map.70), channel_id=2, replica_groups=mesh['zhi'=4,'zlo'=4,'core'=2,'lat'=16] {'zhi'}, dimensions={0}, use_global_device_ids=true | all-gather | bytes 491520 | tf_op jit(solution)/shard_map/all_gather | solution.py:246
  64.4 0.0 copy-done.5
  64.4 0.1 shard_map.71
  64.5 18.3 %all_gather.26.right.acts = bf16[1024,384]{1,0:T(8,128)(2,1)S(1)} all-gather(bf16[128,384]{1,0:T(8,128)(2,1)S(1)} %shard_map.71), channel_id=1, replica_groups=mesh['zhi'=4,'zlo'=4,'core'=2,'lat'=16] {'zlo','core'}, dimensions={0}, use_global_device_ids=true | all-gather | bytes 884736 | tf_op jit(solution)/shard_map/all_gather | solution.py:249
  82.8 0.7 shard_map.72
  83.5 15.6 %all_to_all.26.tiles = bf16[16,32,384]{2,1,0:T(8,128)(2,1)S(1)} all-to-all(bf16[16,32,384]{2,1,0:T(8,128)(2,1)S(1)} %bitcast.33), channel_id=1, replica_groups=mesh['zhi'=4,'zlo'=4,'core'=2,'lat'=16] {'lat'}, dimensions={0} | all-to-all | bytes 786432 | tf_op jit(solution)/shard_map/all_to_all | solution.py:26
  99.1 0.1 shard_map.73
  99.2 11.8 %all_to_all.27 = bf16[16,32,384]{2,1,0:T(8,128)(2,1)S(1)} all-to-all(bf16[16,32,384]{2,1,0:T(8,128)(2,1)S(1)} %shard_map.73), channel_id=1, replica_groups=mesh['zhi'=4,'zlo'=4,'core'=2,'lat'=16] {'lat'}, dimensions={0} | all-to-all | bytes 786432 | tf_op jit(solution)/shard_map/all_to_all | solution.py:26
  111.0 4.6 %all_gather.27.errors = bf16[2,512,384]{2,1,0:T(8,128)(2,1)S(1)} all-gather(bf16[1,512,384]{2,1,0:T(8,128)(2,1)S(1)} %bitcast.25), channel_id=1, replica_groups=mesh['zhi'=4,'zlo'=4,'core'=2,'lat'=16] {'core'}, dimensions={0}, use_global_device_ids=true | all-gather | bytes 1179648 | tf_op jit(solution)/shard_map/all_gather | solution.py:261
  115.6 0.0 copy-done.4
  115.6 2.5 %shard_map.74 = bf16[512,384]{1,0:T(8,128)(2,1)} custom-call(bf16[512,512]{1,0:T(8,128)(2,1)S(1)} %bitcast.29, bf16[512,512]{1,0:T(8,128)(2,1)} %collective-permute-done.got, bf16[2,512,384]{2,1,0:T(8,128)(2,1)S(1)} %all_gather.27.errors), custom_call_target="tpu_custom_call" | custom-call | flops 402653184 | bytes 2228224 | tf_op jit(solution)/shard_map/pallas_call | solution.py:59
  118.1 3.6 %all-to-all-start.4 = ((bf16[4,128,384]{2,1,0:T(8,128)(2,1)}), bf16[4,128,384]{2,1,0:T(8,128)(2,1)S(1)}, u32[]{:S(2)}, u32[]{:S(2)}) async-start(bf16[4,128,384]{2,1,0:T(8,128)(2,1)} %bitcast.12), calls=%async_computation.5 | async-start | bytes 786432 | tf_op jit(solution)/shard_map/all_to_all | solution.py:26
  121.7 0.1 dynamic-slice_bitcast_fusion
  121.8 0.1 copy.18.bias
  121.9 1.3 shard_map.75
  123.2 0.0 copy-start.2
  123.2 1.3 copy-done.2
  124.5 8.6 %all-to-all-done.4.tiles = bf16[4,128,384]{2,1,0:T(8,128)(2,1)S(1)} async-done(((bf16[4,128,384]{2,1,0:T(8,128)(2,1)}), bf16[4,128,384]{2,1,0:T(8,128)(2,1)S(1)}, u32[]{:S(2)}, u32[]{:S(2)}) %all-to-all-start.4) | async-done | bytes 393248 | tf_op jit(solution)/shard_map/all_to_all | solution.py:26
  133.1 0.0 copy-done.7
  133.1 0.1 shard_map.76
  133.2 23.5 %all-gather.1 = bf16[704,384]{1,0:T(8,128)(2,1)S(1)} all-gather(bf16[176,384]{1,0:T(8,128)(2,1)S(1)} %shard_map.76), channel_id=3, replica_groups=mesh['zhi'=4,'zlo'=4,'core'=2,'lat'=16] {'zhi'}, dimensions={0}, use_global_device_ids=true | all-gather | bytes 675840 | tf_op jit(solution)/shard_map/all_gather | solution.py:280
  156.7 0.1 shard_map.77
  156.8 20.1 %all-gather.2 = bf16[1152,384]{1,0:T(8,128)(2,1)S(1)} all-gather(bf16[144,384]{1,0:T(8,128)(2,1)S(1)} %shard_map.77), channel_id=4, replica_groups=mesh['zhi'=4,'zlo'=4,'core'=2,'lat'=16] {'zlo','core'}, dimensions={0}, use_global_device_ids=true | all-gather | bytes 995328 | tf_op jit(solution)/shard_map/all_gather | solution.py:282
  176.9 0.0 copy-done.6
  176.9 2.1 %shard_map.78 = (bf16[512,1024]{1,0:T(8,128)(2,1)}, bf16[1024,512]{1,0:T(8,128)(2,1)}) custom-call(bf16[512,384]{1,0:T(8,128)(2,1)S(1)} %bitcast.31, bf16[8,144,384]{2,1,0:T(8,128)(2,1)S(1)} %bitcast.27, f32[1024,512]{1,0:T(8,128)S(1)} %copy-done.3, bf16[1024,512]{1,0:T(8,128)(2,1)S(1)} %copy-done.1), custom_call_target="tpu_custom_call" | custom-call | flops 402653184 | bytes 6520832 | tf_op jit(solution)/shard_map/pallas_call | solution.py:59
  (7 shorter events, 0.0 us)
Async XLA Ops:
  7.2 26.2 %copy-start = (f32[1024]{0:T(1024)S(1)}, f32[1024]{0:T(1024)}, u32[]{:S(2)}) copy-start(f32[1024]{0:T(1024)} %param.7) | copy-start | bytes 12292
  23.7 4.7 %copy-start.1 = (bf16[1024,512]{1,0:T(8,128)(2,1)S(1)}, bf16[1024,512]{1,0:T(8,128)(2,1)}, u32[]{:S(2)}) copy-start(bf16[1024,512]{1,0:T(8,128)(2,1)} %decoder.3) | copy-start | bytes 3145732
  24.8 14.9 %all-to-all-start.1 = ((bf16[4,128,384]{2,1,0:T(8,128)(2,1)}), bf16[4,128,384]{2,1,0:T(8,128)(2,1)S(1)}, u32[]{:S(2)}, u32[]{:S(2)}) async-start(bf16[4,128,384]{2,1,0:T(8,128)(2,1)} %bitcast.3), calls=%async_computation.1 | async-start | bytes 786432 | tf_op jit(solution)/shard_map/all_to_all | solution.py:26
  28.3 3.4 %copy-start.8 = (bf16[384,512]{1,0:T(8,128)(2,1)S(1)}, bf16[384,512]{1,0:T(8,128)(2,1)}, u32[]{:S(2)}) copy-start(bf16[384,512]{1,0:T(8,128)(2,1)} %residuals.1) | copy-start | bytes 1179652
  28.3 89.8 %reduce-scatter.2.cloned.1.call-start = ((), (), s32[]{:S(2)}) async-start(), calls=%async_computation.6 | async-start | bytes 835584 | tf_op jit(solution)/shard_map/reduce_scatter | solution.py:230
  29.4 10.3 %collective-permute-start = (bf16[512,512]{1,0:T(8,128)(2,1)}, bf16[512,512]{1,0:T(8,128)(2,1)}, u32[]{:S(2)}, u32[]{:S(2)}) collective-permute-start(bf16[512,512]{1,0:T(8,128)(2,1)} %bitcast.6), channel_id=1, source_target_pairs={{0,16},{16,0},{1,17},{17,1},{2,18},{18,2},{3,19},{19,3},{4,20},{20... | collective-permute-start | bytes 1572872 | tf_op jit(solution)/shard_map/ppermute | solution.py:239
  31.9 32.5 %copy-start.5 = (bf16[384,512]{0,1:T(8,128)(2,1)}, bf16[384,512]{0,1:T(8,128)(2,1)S(1)}, u32[]{:S(2)}) copy-start(bf16[384,512]{0,1:T(8,128)(2,1)S(1)} %copy.13) | copy-start | bytes 1179652
  99.1 16.5 %copy-start.4 = (bf16[4,1,128,512]{3,2,1,0:T(8,128)(2,1)S(1)}, bf16[4,1,128,512]{3,2,1,0:T(8,128)(2,1)}, u32[]{:S(2)}) copy-start(bf16[4,1,128,512]{3,2,1,0:T(8,128)(2,1)} %get-tuple-element.27) | copy-start | bytes 1572868
  118.1 15.0 %copy-start.7 = (f32[32,384]{1,0:T(8,128)S(1)}, f32[32,384]{1,0:T(8,128)}, u32[]{:S(2)}) copy-start(f32[32,384]{1,0:T(8,128)} %reduce-scatter.2.cloned.1.call-done.pre) | copy-start | bytes 147460
  118.1 15.0 %all-to-all-start.4 = ((bf16[4,128,384]{2,1,0:T(8,128)(2,1)}), bf16[4,128,384]{2,1,0:T(8,128)(2,1)S(1)}, u32[]{:S(2)}, u32[]{:S(2)}) async-start(bf16[4,128,384]{2,1,0:T(8,128)(2,1)} %bitcast.12), calls=%async_computation.5 | async-start | bytes 786432 | tf_op jit(solution)/shard_map/all_to_all | solution.py:26
  123.2 1.3 copy-start.2
  124.5 52.4 %copy-start.6 = (bf16[384,512]{0,1:T(8,128)(2,1)S(1)}, bf16[384,512]{0,1:T(8,128)(2,1)}, u32[]{:S(2)}) copy-start(bf16[384,512]{0,1:T(8,128)(2,1)} %copy-done.5) | copy-start | bytes 1179652
  133.1 43.8 %copy-start.3 = (f32[1024,512]{1,0:T(8,128)S(1)}, f32[1024,512]{1,0:T(8,128)}, u32[]{:S(2)}) copy-start(f32[1024,512]{1,0:T(8,128)} %copy-done.2) | copy-start | bytes 6291460
Sparse Core Ops, SparseCore 0:
  32.5 61.6 reduce-scatter.1
